TPU v7x, 512 devices: a whole 4x4x16 slice. The times are simulated.
512 devices in a mesh: sim: 128 (over y, z, core), grp: 4 (over x).
Axes of the slice: x: 4, y: 4, z: 16, core: 2. Of those that a mesh axis runs over, the one named last changes fastest.
Arguments:
- species: float32 [2, 512, 128, 1024], P(None, ('sim', 'grp')), may hold values from 0 to 1
Outputs:
- species_next: float32 [2, 512, 128, 1024], P(None, ('sim', 'grp'))
- frame: float32 [4, 256, 2048], P(None, 'sim', 'grp')
All inputs are finite; a program needn't handle non-finite values.
Results may differ from a plain program's by a relative error of at most 0.000034.
Values sent between devices are 32-bit elements; how exact they have to be, the bound alone decides.
A program may use at most 192 MiB of HBM per device.

v0:
```python
import jax
import jax.numpy as jnp
from jax import lax
from jax.sharding import PartitionSpec as P

diff_substrate = 0.16
diff_catalyst = 0.08
feed_rate = 0.035
kill_rate = 0.065


def extended(value, sides, width):
    for axis, dim in sides:
        devices, length = (lax.axis_size(axis), value.shape[dim])
        up = [(i, (i + 1) % devices) for i in range(devices - 1)]
        down = [(j, i) for i, j in up]
        last = lax.slice_in_dim(value, length - width, length, axis=dim)
        first = lax.slice_in_dim(value, 0, width, axis=dim)
        before = lax.ppermute(last, axis, up)
        after = lax.ppermute(first, axis, down)
        value = jnp.concatenate([before, value, after], axis=dim)
    return value


def swapped(value, axis, apart):
    return lax.ppermute(value, axis, [(i, i ^ 1 << apart) for i in range(lax.axis_size(axis))])


def react_diffuse(padded_z):
    padded = jnp.pad(padded_z, ((0, 0), (0, 0), (1, 1), (1, 1)))
    center = padded[:, 1:-1, 1:-1, 1:-1]
    neighbours = padded[:, 2:, 1:-1, 1:-1] + padded[:, :-2, 1:-1, 1:-1]
    neighbours = neighbours + padded[:, 1:-1, 2:, 1:-1] + padded[:, 1:-1, :-2, 1:-1]
    neighbours = neighbours + padded[:, 1:-1, 1:-1, 2:] + padded[:, 1:-1, 1:-1, :-2]
    laplace_term = neighbours - 6.0 * center
    substrate = center[0]
    catalyst = center[1]
    reaction = substrate * catalyst * catalyst
    new_substrate = (
        substrate + diff_substrate * laplace_term[0] - reaction + feed_rate * (1.0 - substrate)
    )
    new_catalyst = (
        catalyst + diff_catalyst * laplace_term[1] + reaction - (feed_rate + kill_rate) * catalyst
    )
    return jnp.stack([new_substrate, new_catalyst])


def refine(values, axis_num):
    length = values.shape[axis_num]
    lower_side = jnp.concatenate(
        [
            lax.slice_in_dim(values, 0, 1, axis=axis_num),
            lax.slice_in_dim(values, 0, length - 1, axis=axis_num),
        ],
        axis_num,
    )
    upper_side = jnp.concatenate(
        [
            lax.slice_in_dim(values, 1, length, axis=axis_num),
            lax.slice_in_dim(values, length - 1, length, axis=axis_num),
        ],
        axis_num,
    )
    even_part = 0.75 * values + 0.25 * lower_side
    odd_part = 0.75 * values + 0.25 * upper_side
    paired = jnp.stack([even_part, odd_part], axis=axis_num + 1)
    new_shape = list(values.shape)
    new_shape[axis_num] = 2 * length
    return paired.reshape(new_shape)


def shade(sample, extinct):
    opacity = 1.0 - jnp.exp(-extinct * sample * sample)
    red_part = jax.nn.sigmoid(6.0 * (sample - 0.5))
    green_part = jnp.exp(-8.0 * (sample - 0.5) * (sample - 0.5))
    blue_part = jax.nn.sigmoid(-6.0 * (sample - 0.3))
    return jnp.stack(
        [opacity * red_part, opacity * green_part, opacity * blue_part, opacity], axis=-3
    )


def over(front_part, back_part):
    return front_part + (1.0 - front_part[..., 3:4, :, :]) * back_part


def shards(species):
    padded_z = extended(species, ((("sim", "grp"), 1),), 1)
    fresh = react_diffuse(padded_z)
    samples = refine(refine(fresh[1], 1), 2)
    grouped = lax.all_to_all(samples, "grp", split_axis=2, concat_axis=0, tiled=True)
    sim_count = lax.axis_size("sim")
    extinct = 6.0 / (grouped.shape[0] * sim_count)
    picture = shade(grouped[0], extinct)
    for layer in range(1, grouped.shape[0]):
        picture = over(picture, shade(grouped[layer], extinct))
    rows_each = picture.shape[1] // sim_count
    columns = picture.shape[2]
    position_sim = lax.axis_index("sim")
    sections = sim_count.bit_length() - 1
    for section in range(sections):
        bit_value = jnp.bitwise_and(jnp.right_shift(position_sim, section), 1)
        rows_now = picture.shape[1]
        groups_now = rows_now // (2 * rows_each)
        split_rows = picture.reshape(4, groups_now, 2, rows_each, columns)
        kept_half = lax.dynamic_index_in_dim(split_rows, bit_value, 2, keepdims=False).reshape(
            4, rows_now // 2, columns
        )
        given_half = lax.dynamic_index_in_dim(split_rows, 1 - bit_value, 2, keepdims=False).reshape(
            4, rows_now // 2, columns
        )
        partner_half = swapped(given_half, "sim", section)
        in_front = bit_value == 0
        front_part = jnp.where(in_front, kept_half, partner_half)
        back_part = jnp.where(in_front, partner_half, kept_half)
        picture = over(front_part, back_part)
    return (fresh, picture)


def solution(mesh):
    placed = (P(None, ("sim", "grp"), None, None),)
    return jax.shard_map(
        shards,
        mesh=mesh,
        in_specs=placed,
        out_specs=(P(None, ("sim", "grp"), None, None), P(None, "sim", "grp")),
        check_vma=False,
    )
```

profile of v0, /device:TPU:1, one launch (start us, length us, event | category | flops | bytes accessed | tf_op | source)
XLA Modules:
  0.0 217.0 jit_solution(3001679784803999466)
XLA Ops:
  0.6 5.9 %collective-permute-start = (f32[2,1,128,1024]{3,2,1,0:T(8,128)}, f32[2,1,128,1024]{3,2,1,0:T(8,128)S(1)}, u32[]{:S(2)}, u32[]{:S(2)}) collective-permute-start(f32[2,1,128,1024]{3,2,1,0:T(8,128)} %param.1), channel_id=1, source_target_pairs={{1,0},{2,1},{3,2},{4,3},{5,4},{6,5},{7,6},{8,7},{9,8},{10,9},{11,1... | collective-permute-start | bytes 3145736 | tf_op jit(solution)/shard_map/ppermute | solution.py:20
  6.6 1.9 collective-permute-start.1
  8.5 21.3 %collective-permute-done = f32[2,1,128,1024]{3,2,1,0:T(8,128)S(1)} collective-permute-done((f32[2,1,128,1024]{3,2,1,0:T(8,128)}, f32[2,1,128,1024]{3,2,1,0:T(8,128)S(1)}, u32[]{:S(2)}, u32[]{:S(2)}) %collective-permute-start) | collective-permute-done | bytes 1048608 | tf_op jit(solution)/shard_map/ppermute | solution.py:20
  29.8 5.5 %collective-permute-done.1 = f32[2,1,128,1024]{3,2,1,0:T(8,128)S(1)} collective-permute-done((f32[2,1,128,1024]{3,2,1,0:T(8,128)}, f32[2,1,128,1024]{3,2,1,0:T(8,128)S(1)}, u32[]{:S(2)}, u32[]{:S(2)}) %collective-permute-start.1) | collective-permute-done | bytes 1048608 | tf_op jit(solution)/shard_map/ppermute | solution.py:19
  35.3 2.9 %select_maximum_fusion = f32[2,3,130,1026]{3,2,1,0:T(8,128)S(1)} fusion(f32[2,1,128,1024]{3,2,1,0:T(8,128)S(1)} %collective-permute-done, f32[2,1,128,1024]{3,2,1,0:T(8,128)} %param.1, f32[2,1,128,1024]{3,2,1,0:T(8,128)S(1)} %collective-permute-done.1), kind=kLoop, calls=%fused_computation.4 | loop fusion | flops 12004200 | bytes 6346848 | tf_op jit(solution)/shard_map/concatenate | solution.py:21
  41.7 2.9 %slice_bitcast_fusion.1 = (f32[1,256,1023,1]{2,0,1,3:T(1,128)S(1)}, f32[1,256,1023,1]{2,0,1,3:T(1,128)S(1)}) fusion(f32[1,256,1024]{2,0,1:T(1,128)S(1)} %bitcast.223), kind=kLoop, calls=%fused_computation.19 | loop fusion | bytes 4190208 | tf_op jit(solution)/shard_map/concatenate | solution.py:50
  46.0 4.2 %fusion.6 = (f32[1,256,1024,1]{2,0,1,3:T(1,128)S(1)}, f32[1,256,1024,1]{2,0,1,3:T(1,128)S(1)}) fusion(f32[1,256,1024,1]{2,0,1,3:T(1,128)S(1)} %bitcast.229, f32[1,256,1023,1]{2,0,1,3:T(1,128)S(1)} %get-tuple-element.39, f32[1,256,1,1]{2,0,1,3:T(1,128)S(1)} %get-tuple-element.37, f32[1,256,1,1]{2,0,1,3:T(1,128)S(1)} %get-tuple-element.38, ...), kind=kLoop, calls=%fused_computation.28 | loop fusion | flops 1572864 | bytes 5242880 | tf_op jit(solution)/shard_map/add | solution.py:64
  50.2 1.8 pad_maximum_fusion
  52.0 5.7 %copy.46 = f32[1,256,1024,2]{1,0,3,2:T(1,128)} copy(f32[1,256,1024,2]{2,0,1,3:T(1,128)S(1)} %pad_maximum_fusion) | data formatting | bytes 4194304 | tf_op jit(solution)/shard_map/stack | solution.py:66
  57.7 3.6 %all-to-all-start = ((f32[1,256,2048]{1,0,2:T(1,128)}), f32[1,256,2048]{1,0,2:T(1,128)S(1)}, u32[]{:S(2)}, u32[]{:S(2)}) async-start(f32[1,256,2048]{1,0,2:T(1,128)} %bitcast.226), calls=%async_computation | async-start | bytes 4194304 | tf_op jit(solution)/shard_map/all_to_all | solution.py:90
  61.4 23.9 %all-to-all-done = f32[1,256,2048]{1,0,2:T(1,128)S(1)} async-done(((f32[1,256,2048]{1,0,2:T(1,128)}), f32[1,256,2048]{1,0,2:T(1,128)S(1)}, u32[]{:S(2)}, u32[]{:S(2)}) %all-to-all-start) | async-done | bytes 2097184 | tf_op jit(solution)/shard_map/all_to_all | solution.py:90
  86.6 4.8 %copy.47 = f32[1,256,4,512]{3,2,1,0:T(4,128)S(1)} copy(f32[1,256,4,512]{1,0,3,2:T(1,128)} %bitcast.225) | data formatting | bytes 4194304 | tf_op jit(solution)/shard_map/all_to_all | solution.py:90
  91.4 2.0 divide_multiply_fusion.1
  93.4 4.9 %slice_reduce_fusion = (f32[256,512]{1,0:T(8,128)}, f32[1,1,256,512]{3,0,2,1:T(1,128)}, f32[1,1,256,512]{3,0,2,1:T(1,128)}, f32[1,1,256,512]{3,0,2,1:T(1,128)}, f32[1,1,256,512]{3,0,2,1:T(1,128)S(1)}) fusion(f32[4,1,256,512]{3,0,2,1:T(4,128)S(1)} %bitcast.220), kind=kLoop, calls=%fused_computation.208 | loop fusion | bytes 4718592 | tf_op jit(solution)/shard_map/slice | solution.py:93
  98.2 5.7 %fusion.44 = (f32[1,256,512]{2,0,1:T(1,128)S(1)}, f32[1,256,512]{2,0,1:T(1,128)S(1)}, f32[1,256,512]{2,0,1:T(1,128)S(1)}, f32[1,256,512]{2,0,1:T(1,128)S(1)}, f3...) fusion(f32[1,256,512]{2,0,1:T(1,128)S(1)} %get-tuple-element.5, f32[4,1,256,512]{3,0,2,1:T(4,128)S(1)} %bitcast.221), kind=kLoop, calls=%fused_computation.94 | loop fusion | flops 3670016 | bytes 5242880 | tf_op jit(solution)/shard_map/mul | solution.py:78
  104.1 3.9 %fusion.36 = (f32[1,256,512]{2,0,1:T(1,128)S(1)}, f32[1,256,512]{2,0,1:T(1,128)S(1)}, f32[1,256,512]{2,0,1:T(1,128)S(1)}, f32[1,256,512]{2,0,1:T(1,128)S(1)}) fusion(f32[1,256,512]{2,0,1:T(1,128)S(1)} %get-tuple-element.26, f32[4,1,256,512]{3,0,2,1:T(4,128)S(1)} %bitcast.222, f32[1,256,512]{2,0,1:T(1,128)S(1)} %get-tuple-element.24), kind=kLoop, calls=%fused_computation.86 | loop fusion | flops 2621440 | bytes 4194304 | tf_op jit(solution)/shard_map/mul | solution.py:78
  108.0 4.2 %maximum_add_fusion.1 = f32[4,256,512]{2,0,1:T(4,128)S(1)} fusion(f32[1,256,512]{2,0,1:T(1,128)S(1)} %get-tuple-element.24, f32[1,256,512]{2,0,1:T(1,128)S(1)} %get-tuple-element.27, f32[1,256,512]{2,0,1:T(1,128)S(1)} %get-tuple-element.28, f32[1,256,512]{2,0,1:T(1,128)S(1)} %get-tuple-element.23, f32[1,256,512]{2,0,1:T(1,128)S(1)} %get-tuple-element.26, ...), kind=kLoop, calls=%fused_computation.14 | loop fusion | flops 4194304 | bytes 6815744 | tf_op jit(solution)/shard_map/add | solution.py:83
  112.9 5.3 %fusion.81 = (f32[256,512]{1,0:T(8,128)S(1)}, f32[256,512]{1,0:T(8,128)S(1)}) fusion(f32[4,256,512]{2,0,1:T(4,128)S(1)} %maximum_add_fusion.1, f32[1,256,512]{2,0,1:T(1,128)S(1)} %get-tuple-element.5, f32[1,256,512]{2,0,1:T(1,128)S(1)} %get-tuple-element.11, f32[1,256,512]{2,0,1:T(1,128)S(1)} %get-tuple-element.10, f32[1,256,512]{2,0,1:T(1,128)S(1)} %get-tuple-element.4, ...), kind=kLoop, calls=%fused_computation.207 | loop fusion | flops 917504 | bytes 4194304 | tf_op jit(solution)/shard_map/sub | solution.py:83
  119.8 2.1 copy.62
  128.4 1.7 copy.68
  130.0 1.9 collective-permute-start.2
  132.6 2.1 collective-permute-done.2
  136.0 4.3 %collective-permute-start.3 = (f32[4,64,512]{2,0,1:T(4,128)S(1)}, f32[4,64,512]{2,0,1:T(4,128)S(1)}, u32[]{:S(2)}, u32[]{:S(2)}) collective-permute-start(f32[4,64,512]{2,0,1:T(4,128)S(1)} %bitcast.239), channel_id=1, source_target_pairs={{0,8},{4,12},{8,0},{12,4},{16,24},{20,28},{24,16},{28,20},{32,40},... | collective-permute-start | bytes 1572872 | tf_op jit(solution)/shard_map/ppermute | solution.py:26
  140.3 12.1 %collective-permute-done.3 = f32[4,64,512]{2,0,1:T(4,128)S(1)} collective-permute-done((f32[4,64,512]{2,0,1:T(4,128)S(1)}, f32[4,64,512]{2,0,1:T(4,128)S(1)}, u32[]{:S(2)}, u32[]{:S(2)}) %collective-permute-start.3) | collective-permute-done | bytes 524320 | tf_op jit(solution)/shard_map/ppermute | solution.py:26
  153.1 4.9 %collective-permute-start.4 = (f32[4,32,512]{2,0,1:T(4,128)S(1)}, f32[4,32,512]{2,0,1:T(4,128)S(1)}, u32[]{:S(2)}, u32[]{:S(2)}) collective-permute-start(f32[4,32,512]{2,0,1:T(4,128)S(1)} %bitcast.240), channel_id=1, source_target_pairs={{0,16},{4,20},{8,24},{12,28},{16,0},{20,4},{24,8},{28,12},{32,48},... | collective-permute-start | bytes 786440 | tf_op jit(solution)/shard_map/ppermute | solution.py:26
  158.0 11.5 %collective-permute-done.4 = f32[4,32,512]{2,0,1:T(4,128)S(1)} collective-permute-done((f32[4,32,512]{2,0,1:T(4,128)S(1)}, f32[4,32,512]{2,0,1:T(4,128)S(1)}, u32[]{:S(2)}, u32[]{:S(2)}) %collective-permute-start.4) | collective-permute-done | bytes 262176 | tf_op jit(solution)/shard_map/ppermute | solution.py:26
  169.9 8.8 %collective-permute-start.5 = (f32[4,16,512]{2,0,1:T(4,128)S(1)}, f32[4,16,512]{2,0,1:T(4,128)S(1)}, u32[]{:S(2)}, u32[]{:S(2)}) collective-permute-start(f32[4,16,512]{2,0,1:T(4,128)S(1)} %bitcast.244), channel_id=1, source_target_pairs={{0,32},{4,36},{8,40},{12,44},{16,48},{20,52},{24,56},{28,60},{32,0... | collective-permute-start | bytes 393224 | tf_op jit(solution)/shard_map/ppermute | solution.py:26
  178.8 11.3 %collective-permute-done.5 = f32[4,16,512]{2,0,1:T(4,128)S(1)} collective-permute-done((f32[4,16,512]{2,0,1:T(4,128)S(1)}, f32[4,16,512]{2,0,1:T(4,128)S(1)}, u32[]{:S(2)}, u32[]{:S(2)}) %collective-permute-start.5) | collective-permute-done | bytes 131104 | tf_op jit(solution)/shard_map/ppermute | solution.py:26
  190.3 13.2 %collective-permute-start.6 = (f32[4,8,512]{2,0,1:T(4,128)S(1)}, f32[4,8,512]{2,0,1:T(4,128)S(1)}, u32[]{:S(2)}, u32[]{:S(2)}) collective-permute-start(f32[4,8,512]{2,0,1:T(4,128)S(1)} %bitcast.246), channel_id=1, source_target_pairs={{0,64},{4,68},{8,72},{12,76},{16,80},{20,84},{24,88},{28,92},{32,9... | collective-permute-start | bytes 196616 | tf_op jit(solution)/shard_map/ppermute | solution.py:26
  203.5 2.0 collective-permute-done.6
  205.6 3.2 %collective-permute-start.7 = (f32[4,4,512]{2,0,1:T(4,128)S(1)}, f32[4,4,512]{2,0,1:T(4,128)S(1)}, u32[]{:S(2)}, u32[]{:S(2)}) collective-permute-start(f32[4,4,512]{2,0,1:T(4,128)S(1)} %bitcast.248), channel_id=1, source_target_pairs={{0,128},{4,132},{8,136},{12,140},{16,144},{20,148},{24,152},{28,15... | collective-permute-start | bytes 98312 | tf_op jit(solution)/shard_map/ppermute | solution.py:26
  210.4 4.8 %collective-permute-start.8 = (f32[4,2,512]{2,1,0:T(2,128)S(1)}, f32[4,2,512]{2,1,0:T(2,128)S(1)}, u32[]{:S(2)}, u32[]{:S(2)}) collective-permute-start(f32[4,2,512]{2,1,0:T(2,128)S(1)} %bitcast.250), channel_id=1, source_target_pairs={{0,256},{4,260},{8,264},{12,268},{16,272},{20,276},{24,280},{28,28... | collective-permute-start | bytes 49160 | tf_op jit(solution)/shard_map/ppermute | solution.py:26
  (83 shorter events, 21.4 us)
Async XLA Ops:
  0.6 37.6 %copy-start = (f32[2,1,128,1024]{3,2,1,0:T(8,128)S(1)}, f32[2,1,128,1024]{3,2,1,0:T(8,128)}, u32[]{:S(2)}) copy-start(f32[2,1,128,1024]{3,2,1,0:T(8,128)} %param.1) | copy-start | bytes 3145732
  0.6 29.2 %collective-permute-start = (f32[2,1,128,1024]{3,2,1,0:T(8,128)}, f32[2,1,128,1024]{3,2,1,0:T(8,128)S(1)}, u32[]{:S(2)}, u32[]{:S(2)}) collective-permute-start(f32[2,1,128,1024]{3,2,1,0:T(8,128)} %param.1), channel_id=1, source_target_pairs={{1,0},{2,1},{3,2},{4,3},{5,4},{6,5},{7,6},{8,7},{9,8},{10,9},{11,1... | collective-permute-start | bytes 3145736 | tf_op jit(solution)/shard_map/ppermute | solution.py:20
  6.6 28.8 %collective-permute-start.1 = (f32[2,1,128,1024]{3,2,1,0:T(8,128)}, f32[2,1,128,1024]{3,2,1,0:T(8,128)S(1)}, u32[]{:S(2)}, u32[]{:S(2)}) collective-permute-start(f32[2,1,128,1024]{3,2,1,0:T(8,128)} %param.1), channel_id=1, source_target_pairs={{0,1},{1,2},{2,3},{3,4},{4,5},{5,6},{6,7},{7,8},{8,9},{9,10},{10,1... | collective-permute-start | bytes 3145736 | tf_op jit(solution)/shard_map/ppermute | solution.py:19
  39.2 1.0 copy-start.1
  57.7 27.5 %all-to-all-start = ((f32[1,256,2048]{1,0,2:T(1,128)}), f32[1,256,2048]{1,0,2:T(1,128)S(1)}, u32[]{:S(2)}, u32[]{:S(2)}) async-start(f32[1,256,2048]{1,0,2:T(1,128)} %bitcast.226), calls=%async_computation | async-start | bytes 4194304 | tf_op jit(solution)/shard_map/all_to_all | solution.py:90
  85.3 1.3 copy-start.3
  98.2 5.7 %copy-start.4 = (f32[1,1,256,512]{3,0,2,1:T(1,128)}, f32[1,1,256,512]{3,0,2,1:T(1,128)S(1)}, u32[]{:S(2)}) copy-start(f32[1,1,256,512]{3,0,2,1:T(1,128)S(1)} %get-tuple-element.22) | copy-start | bytes 1572868
  118.2 3.7 %copy-start.9 = (f32[256,512]{1,0:T(8,128)S(1)}, f32[256,512]{1,0:T(8,128)}, u32[]{:S(2)}) copy-start(f32[256,512]{1,0:T(8,128)} %get-tuple-element.18) | copy-start | bytes 1572868
  119.8 4.9 %copy-start.7 = (f32[1,1,256,512]{3,0,2,1:T(1,128)S(1)}, f32[1,1,256,512]{3,0,2,1:T(1,128)}, u32[]{:S(2)}) copy-start(f32[1,1,256,512]{3,0,2,1:T(1,128)} %get-tuple-element.19) | copy-start | bytes 1572868
  119.8 4.9 %copy-start.8 = (f32[1,1,256,512]{3,0,2,1:T(1,128)S(1)}, f32[1,1,256,512]{3,0,2,1:T(1,128)}, u32[]{:S(2)}) copy-start(f32[1,1,256,512]{3,0,2,1:T(1,128)} %get-tuple-element.20) | copy-start | bytes 1572868
  124.7 1.0 copy-start.5
  124.7 1.2 copy-start.6
  125.9 1.0 copy-start.10
  130.0 4.8 %collective-permute-start.2 = (f32[4,128,512]{2,0,1:T(4,128)}, f32[4,128,512]{2,0,1:T(4,128)S(1)}, u32[]{:S(2)}, u32[]{:S(2)}) collective-permute-start(f32[4,128,512]{2,0,1:T(4,128)} %bitcast.27), channel_id=1, source_target_pairs={{0,4},{4,0},{8,12},{12,8},{16,20},{20,16},{24,28},{28,24},{32,36},... | collective-permute-start | bytes 3145736 | tf_op jit(solution)/shard_map/ppermute | solution.py:26
  136.0 16.4 %collective-permute-start.3 = (f32[4,64,512]{2,0,1:T(4,128)S(1)}, f32[4,64,512]{2,0,1:T(4,128)S(1)}, u32[]{:S(2)}, u32[]{:S(2)}) collective-permute-start(f32[4,64,512]{2,0,1:T(4,128)S(1)} %bitcast.239), channel_id=1, source_target_pairs={{0,8},{4,12},{8,0},{12,4},{16,24},{20,28},{24,16},{28,20},{32,40},... | collective-permute-start | bytes 1572872 | tf_op jit(solution)/shard_map/ppermute | solution.py:26
  153.1 16.4 %collective-permute-start.4 = (f32[4,32,512]{2,0,1:T(4,128)S(1)}, f32[4,32,512]{2,0,1:T(4,128)S(1)}, u32[]{:S(2)}, u32[]{:S(2)}) collective-permute-start(f32[4,32,512]{2,0,1:T(4,128)S(1)} %bitcast.240), channel_id=1, source_target_pairs={{0,16},{4,20},{8,24},{12,28},{16,0},{20,4},{24,8},{28,12},{32,48},... | collective-permute-start | bytes 786440 | tf_op jit(solution)/shard_map/ppermute | solution.py:26
  169.6 39.3 %copy-start.2 = (f32[2,1,128,1024]{3,2,1,0:T(8,128)S(1)}, f32[2,1,128,1024]{3,2,1,0:T(8,128)}, u32[]{:S(2)}) copy-start(f32[2,1,128,1024]{3,2,1,0:T(8,128)} %copy-done.1) | copy-start | bytes 3145732
  169.9 20.2 %collective-permute-start.5 = (f32[4,16,512]{2,0,1:T(4,128)S(1)}, f32[4,16,512]{2,0,1:T(4,128)S(1)}, u32[]{:S(2)}, u32[]{:S(2)}) collective-permute-start(f32[4,16,512]{2,0,1:T(4,128)S(1)} %bitcast.244), channel_id=1, source_target_pairs={{0,32},{4,36},{8,40},{12,44},{16,48},{20,52},{24,56},{28,60},{32,0... | collective-permute-start | bytes 393224 | tf_op jit(solution)/shard_map/ppermute | solution.py:26
  190.3 15.2 %collective-permute-start.6 = (f32[4,8,512]{2,0,1:T(4,128)S(1)}, f32[4,8,512]{2,0,1:T(4,128)S(1)}, u32[]{:S(2)}, u32[]{:S(2)}) collective-permute-start(f32[4,8,512]{2,0,1:T(4,128)S(1)} %bitcast.246), channel_id=1, source_target_pairs={{0,64},{4,68},{8,72},{12,76},{16,80},{20,84},{24,88},{28,92},{32,9... | collective-permute-start | bytes 196616 | tf_op jit(solution)/shard_map/ppermute | solution.py:26
  205.6 4.7 %collective-permute-start.7 = (f32[4,4,512]{2,0,1:T(4,128)S(1)}, f32[4,4,512]{2,0,1:T(4,128)S(1)}, u32[]{:S(2)}, u32[]{:S(2)}) collective-permute-start(f32[4,4,512]{2,0,1:T(4,128)S(1)} %bitcast.248), channel_id=1, source_target_pairs={{0,128},{4,132},{8,136},{12,140},{16,144},{20,148},{24,152},{28,15... | collective-permute-start | bytes 98312 | tf_op jit(solution)/shard_map/ppermute | solution.py:26
  210.4 6.0 %collective-permute-start.8 = (f32[4,2,512]{2,1,0:T(2,128)S(1)}, f32[4,2,512]{2,1,0:T(2,128)S(1)}, u32[]{:S(2)}, u32[]{:S(2)}) collective-permute-start(f32[4,2,512]{2,1,0:T(2,128)S(1)} %bitcast.250), channel_id=1, source_target_pairs={{0,256},{4,260},{8,264},{12,268},{16,272},{20,276},{24,280},{28,28... | collective-permute-start | bytes 49160 | tf_op jit(solution)/shard_map/ppermute | solution.py:26
where the time goes:
time: 220 us; the launch traced here: 217 us
  waiting for transfers between devices  91.2 us (41%)
  starting transfers between devices  52.5 us (24%)
  other arithmetic  41.1 us (19%)
  local copies, waits for them, and re-layouts  30.9 us (14%)
    ppermute x7, starting transfers between devices, swapped(): lax.ppermute(value, axis, [(i, i ^ 1 << apart) for i in range(lax.axis_si...  41.1 us
    ppermute x7, waiting for transfers between devices, swapped(): lax.ppermute(value, axis, [(i, i ^ 1 << apart) for i in range(lax.axis_si...  40.5 us
    all_to_all x1, waiting for transfers between devices, shards(): lax.all_to_all(samples, 'grp', split_axis=2, concat_axis=0, tiled=True)  23.9 us
    ppermute x1, waiting for transfers between devices, extended(): after = lax.ppermute(first, axis, down)  21.3 us
    mul x2, other arithmetic, shade(): opacity * green_part  9.63 us
    sub x10, other arithmetic, over(): return front_part + (1.0 - front_part[..., 3:4, :, :]) * back_part  8.22 us
    add x9, other arithmetic, over(): return front_part + (1.0 - front_part[..., 3:4, :, :]) * back_part  6.94 us
    another operation x2, local copies, waits for them, and re-layouts, refine(): paired = jnp.stack([even_part, odd_part], axis=axis_num + 1)  6.77 us
  transfers between devices with their start and end apart: 10, of which 10 were waited for; matrix products, arithmetic and copies ran while one was open for 1% of the time, Pallas kernels for 0%

commit v1 on v0

v1 whole, which is shorter than its diff:
```python
import jax
import jax.numpy as jnp
from jax import lax
from jax.experimental import pallas as pl
from jax.experimental.pallas import tpu as pltpu
from jax.sharding import PartitionSpec as P

MESH = pl.DeviceIdType.MESH

ROWS = 128
COLS = 1024
GRP = 4
SIMS = 128
SUB = 8
BLOCKS = SIMS // SUB
MEMBERS = GRP * SUB
REGION = ROWS // SUB
CHUNKS = 8
CHUNK = ROWS // CHUNKS
SLOT = 40
PIECE = 32

DIFF_S, DIFF_C, FEED, KILL = 0.16, 0.08, 0.035, 0.065


def to(sim, grp):
    return {"sim": sim, "grp": grp}


def laplacian(buf, up, dn, r):
    window = buf[pl.ds(r, 24), :]
    center = window[8:16]
    lane = lax.broadcasted_iota(jnp.int32, (8, COLS), 1)
    left = jnp.where(lane == 0, 0.0, pltpu.roll(center, 1, 1))
    right = jnp.where(lane == COLS - 1, 0.0, pltpu.roll(center, COLS - 1, 1))
    total = up[pl.ds(r, 8), :] + dn[pl.ds(r, 8), :]
    total = total + window[7:15] + window[9:17] + left + right
    return center, total - 6.0 * center


def kernel(
    species, next_out, frame_out,
    sbuf, cbuf, s_up, s_dn, c_up, c_dn, s_new, c_new, edge_cols, sendbuf, recvbuf, pack, parts,
    load_sem, store_sem, halo_send, halo_recv, own_sem, mix_send, mix_recv, part_own, part_send, part_recv,
):
    sim, grp = lax.axis_index("sim"), lax.axis_index("grp")
    plane = sim * GRP + grp
    block, member = lax.div(sim, SUB), lax.rem(sim, SUB)
    seat = member * GRP + grp
    turn = lax.div(block, 4) + lax.rem(block, 4)

    def region_of(m, turn):
        return 2 * lax.rem(lax.div(m, 2) + 8 - turn, 4) + lax.rem(m, 2)

    def member_of(q, turn):
        return 2 * lax.rem(lax.div(q, 2) + turn, 4) + lax.rem(q, 2)

    region = region_of(member, turn)

    def source(b):
        t = lax.div(b, 4) + lax.rem(b, 4)
        return b * SUB + member_of(lax.div(sim, REGION), t)

    loads = [
        pltpu.make_async_copy(species.at[i, 0], buf.at[pl.ds(8, ROWS), :], load_sem.at[i])
        for i, buf in ((0, sbuf), (1, cbuf))
    ]
    loads[1].start()
    loads[0].start()

    has_prev, has_next = plane > 0, plane < SIMS * GRP - 1
    prev = to(lax.div(plane - 1, GRP), lax.rem(plane - 1 + GRP, GRP))
    nxt = to(lax.div(plane + 1, GRP), lax.rem(plane + 1, GRP))
    barrier = pltpu.get_barrier_semaphore()

    @pl.when(has_prev)
    def _():
        pl.semaphore_signal(barrier, inc=1, device_id=prev, device_id_type=MESH)

    @pl.when(has_next)
    def _():
        pl.semaphore_signal(barrier, inc=1, device_id=nxt, device_id_type=MESH)

    def greet_member(d, _):
        other = lax.rem(seat + d, MEMBERS)
        there = to(block * SUB + lax.div(other, GRP), lax.rem(other, GRP))
        pl.semaphore_signal(barrier, inc=1, device_id=there, device_id_type=MESH)
        return 0

    lax.fori_loop(1, MEMBERS, greet_member, 0)

    def greet_source(b, _):
        there = source(b)

        @pl.when(there != sim)
        def _():
            pl.semaphore_signal(barrier, inc=1, device_id=to(there, grp), device_id_type=MESH)

        return 0

    lax.fori_loop(0, BLOCKS, greet_source, 0)

    for buf in (sbuf, cbuf):
        buf[0:8, :] = jnp.zeros((8, COLS), jnp.float32)
        buf[ROWS + 8 : ROWS + 16, :] = jnp.zeros((8, COLS), jnp.float32)

    @pl.when(plane == 0)
    def _():
        s_up[...] = jnp.zeros_like(s_up)
        c_up[...] = jnp.zeros_like(c_up)

    @pl.when(plane == SIMS * GRP - 1)
    def _():
        s_dn[...] = jnp.zeros_like(s_dn)
        c_dn[...] = jnp.zeros_like(c_dn)

    self_part = lax.div(sim, REGION) == region
    expected = MEMBERS - 1 + BLOCKS - self_part.astype(jnp.int32)
    expected = expected + has_prev.astype(jnp.int32) + has_next.astype(jnp.int32)
    pl.semaphore_wait(barrier, expected)

    def halo(i, way, rows):
        target = ((s_up, s_dn), (c_up, c_dn))[i][way]
        return lambda chunk: pltpu.make_async_remote_copy(
            src_ref=species.at[i, 0, rows, :],
            dst_ref=target.at[rows, :],
            send_sem=halo_send.at[i, way],
            recv_sem=halo_recv.at[i, way, chunk],
            device_id=(nxt, prev)[way],
            device_id_type=MESH,
        )

    def chunk_rows(k):
        return pl.ds(pl.multiple_of(k * CHUNK, CHUNK), CHUNK)

    whole = pl.ds(0, ROWS)

    def send_catalyst(k, _):
        @pl.when(has_next)
        def _():
            halo(1, 0, chunk_rows(k))(k).start()

        @pl.when(has_prev)
        def _():
            halo(1, 1, chunk_rows(k))(k).start()

        return 0

    lax.fori_loop(0, CHUNKS, send_catalyst, 0)
    loads[1].wait()

    loads[0].wait()
    lane = lax.broadcasted_iota(jnp.int32, (8, 128), 1)
    beside = [(0, 0), (2, 0), (1, 127), (4, 0), (3, 127), (6, 0), (5, 127), (7, 127)]

    def catalyst_chunk(k, _):
        @pl.when(has_prev)
        def _():
            halo(1, 0, chunk_rows(k))(k).wait_recv()

        @pl.when(has_next)
        def _():
            halo(1, 1, chunk_rows(k))(k).wait_recv()

        for h in range(CHUNK // 8):
            r = pl.multiple_of(k * CHUNK + 8 * h, 8)
            c, lap = laplacian(cbuf, c_up, c_dn, r)
            s = sbuf[pl.ds(pl.multiple_of(r + 8, 8), 8), :]
            new = c + DIFF_C * lap + s * c * c - (FEED + KILL) * c
            c_new[pl.ds(r, 8), :] = new
            columns = jnp.zeros((8, 128), jnp.float32)
            for n, (tile, at) in enumerate(beside):
                moved = pltpu.roll(new[:, tile * 128 : tile * 128 + 128], (n - at) % 128, 1)
                columns = jnp.where(lane == n, moved, columns)
            edge_cols[pl.ds(r, 8), :] = columns
            for tile in range(COLS // 128):
                slot = (k * GRP + tile // 2) * SLOT + (h * 2 + tile % 2) * 8
                sendbuf[pl.ds(pl.multiple_of(slot, 8), 8), :] = new[:, tile * 128 : tile * 128 + 128]
        return 0

    lax.fori_loop(0, CHUNKS, catalyst_chunk, 0)

    store_c = pltpu.make_async_copy(c_new, next_out.at[1, 0], store_sem.at[1])
    store_c.start()

    beside_t = jnp.transpose(edge_cols[...])[0:8]

    for q in range(SUB):
        above, below = max(q * REGION - 1, 0), min(q * REGION + REGION, ROWS - 1)
        cols = pltpu.roll(beside_t, (1 - q * REGION) % ROWS, 1)
        if q == 0:
            cols = jnp.where(lane == 0, beside_t, cols)
        if q == SUB - 1:
            cols = jnp.where(lane == REGION + 1, pltpu.roll(beside_t, REGION + 2, 1), cols)
        for x in range(GRP):
            base = (q * GRP + x) * SLOT + 32
            for t in range(2):
                col = (2 * x + t) * 128
                sendbuf[base + t : base + t + 1, :] = c_new[above : above + 1, col : col + 128]
                sendbuf[base + 2 + t : base + 3 + t, :] = c_new[below : below + 1, col : col + 128]
            sendbuf[base + 4 : base + 6, :] = cols[2 * x : 2 * x + 2]
            sendbuf[base + 6 : base + 8, :] = jnp.zeros((2, 128), jnp.float32)

    def slot_rows(n):
        return pl.ds(pl.multiple_of(n * SLOT, SLOT), SLOT)

    def mix(other):
        m, x = lax.div(other, GRP), lax.rem(other, GRP)
        return pltpu.make_async_remote_copy(
            src_ref=sendbuf.at[slot_rows(region_of(m, turn) * GRP + x), :],
            dst_ref=recvbuf.at[slot_rows(seat), :],
            send_sem=mix_send,
            recv_sem=mix_recv,
            device_id=to(block * SUB + m, x),
            device_id_type=MESH,
        )

    def send_region(d, _):
        mix(lax.rem(seat + d, MEMBERS)).start()
        return 0

    lax.fori_loop(1, MEMBERS, send_region, 0)
    own = pltpu.make_async_copy(
        sendbuf.at[slot_rows(region * GRP + grp), :], recvbuf.at[slot_rows(seat), :], own_sem
    )
    own.start()

    @pl.when(has_next)
    def _():
        halo(0, 0, whole)(0).start()

    @pl.when(has_prev)
    def _():
        halo(0, 1, whole)(0).start()

    own.wait()
    others = pl.ds(0, (MEMBERS - 1) * SLOT)
    all_mixed = pltpu.make_async_remote_copy(
        src_ref=sendbuf.at[others, :], dst_ref=recvbuf.at[others, :],
        send_sem=mix_send, recv_sem=mix_recv, device_id=to(sim, grp), device_id_type=MESH,
    )
    all_mixed.wait_recv()

    sides = jnp.concatenate(
        [
            recvbuf[pl.ds(36, MEMBERS, stride=SLOT), :],
            recvbuf[pl.ds(37, MEMBERS, stride=SLOT), :],
            jnp.zeros((128 - 2 * MEMBERS, 128), jnp.float32),
        ],
        axis=0,
    )
    sides = jnp.transpose(sides)
    row = lax.broadcasted_iota(jnp.int32, (8, 128), 0)
    extinct = 6.0 / (BLOCKS * MEMBERS)

    for h in range(2):
        for par in range(2):
            near = 2 * par
            side = 0.75 * sides[1 + 8 * h : 9 + 8 * h] + 0.25 * sides[near + 8 * h : near + 8 * h + 8]

            def layer(p, totals, h=h, par=par, side=side):
                base = pl.multiple_of(p * SLOT, 8)
                rim = recvbuf[pl.ds(base + 32, 8), :]
                rows = []
                for t in range(2):
                    mine = recvbuf[pl.ds(base + (2 * h + t) * 8, 8), :]
                    across = recvbuf[pl.ds(base + (2 - 2 * h + t) * 8, 8), :]
                    if par == 0:
                        beyond = rim[t : t + 1] if h == 0 else across[7:8]
                        shifted = jnp.where(row == 0, beyond, pltpu.roll(mine, 1, 0))
                    else:
                        beyond = rim[2 + t : 3 + t] if h == 1 else across[0:1]
                        shifted = jnp.where(row == 7, beyond, pltpu.roll(mine, 7, 0))
                    rows.append(0.75 * mine + 0.25 * shifted)
                leftmost = pltpu.roll(side, lax.rem(128 - p, 128), 1)
                rightmost = pltpu.roll(side, 127 - MEMBERS - p, 1)
                fwd = [pltpu.roll(v, 1, 1) for v in rows]
                bwd = [pltpu.roll(v, 127, 1) for v in rows]
                low = [jnp.where(lane == 0, leftmost, fwd[0]), jnp.where(lane == 0, fwd[0], fwd[1])]
                high = [jnp.where(lane == 127, bwd[1], bwd[0]), jnp.where(lane == 127, rightmost, bwd[1])]
                result = []
                for cpar in range(2):
                    for t in range(2):
                        q = 0.75 * rows[t] + 0.25 * (low, high)[cpar][t]
                        red, green, blue, clear = totals[(cpar * 2 + t) * 4 : (cpar * 2 + t) * 4 + 4]
                        after = clear * jnp.exp(-extinct * (q * q))
                        weight = clear - after
                        mid = q - 0.5
                        red = red + weight * jnp.tanh(3.0 * mid)
                        green = green + weight * jnp.exp(-8.0 * (mid * mid))
                        blue = blue + weight * jnp.tanh(3.0 * (q - 0.3))
                        result += [red, green, blue, after]
                return tuple(result)

            zero, one = jnp.zeros((8, 128), jnp.float32), jnp.ones((8, 128), jnp.float32)
            totals = lax.fori_loop(0, MEMBERS, layer, (zero, zero, zero, one) * 4)
            for cpar in range(2):
                for t in range(2):
                    for ch in range(4):
                        at = 8 * h * PIECE + ch * 8 + cpar * 4 + par * 2 + t
                        pack[pl.ds(at, 8, stride=PIECE), :] = totals[(cpar * 2 + t) * 4 + ch]

    def piece_rows(n):
        return pl.ds(pl.multiple_of(n * PIECE, PIECE), PIECE)

    def send_piece(n, _):
        j = lax.rem(n + sim, REGION)
        there = region * REGION + j

        @pl.when(there != sim)
        def _():
            pltpu.make_async_remote_copy(
                src_ref=pack.at[piece_rows(j), :],
                dst_ref=parts.at[piece_rows(block), :],
                send_sem=part_send,
                recv_sem=part_recv,
                device_id=to(there, grp),
                device_id_type=MESH,
            ).start()

        return 0

    lax.fori_loop(0, REGION, send_piece, 0)

    @pl.when(self_part)
    def _():
        mine = pltpu.make_async_copy(
            pack.at[piece_rows(lax.rem(sim, REGION)), :], parts.at[piece_rows(block), :], part_own
        )
        mine.start()
        mine.wait()

    @pl.when(has_prev)
    def _():
        halo(0, 0, whole)(0).wait_recv()

    @pl.when(has_next)
    def _():
        halo(0, 1, whole)(0).wait_recv()

    def substrate_rows(k, _):
        r = pl.multiple_of(8 * k, 8)
        s, lap = laplacian(sbuf, s_up, s_dn, r)
        c = cbuf[pl.ds(pl.multiple_of(r + 8, 8), 8), :]
        s_new[pl.ds(r, 8), :] = s + DIFF_S * lap - s * c * c + FEED * (1.0 - s)
        return 0

    lax.fori_loop(0, ROWS // 8, substrate_rows, 0)
    store_s = pltpu.make_async_copy(s_new, next_out.at[0, 0], store_sem.at[0])
    store_s.start()

    def wait_parts(count):
        some = pl.ds(0, count * PIECE)
        return pltpu.make_async_remote_copy(
            src_ref=pack.at[some, :], dst_ref=parts.at[some, :],
            send_sem=part_send, recv_sem=part_recv, device_id=to(sim, grp), device_id_type=MESH,
        )

    @pl.when(self_part)
    def _():
        wait_parts(BLOCKS - 1).wait_recv()

    @pl.when(jnp.logical_not(self_part))
    def _():
        wait_parts(BLOCKS).wait_recv()

    def add_block(b, totals):
        base = pl.multiple_of(b * PIECE, 8)
        red, green, blue, clear = totals
        got = [parts[pl.ds(base + 8 * ch, 8), :] for ch in range(4)]
        return (
            red + clear * got[0], green + clear * got[1], blue + clear * got[2], clear * got[3],
        )

    zero, one = jnp.zeros((8, 128), jnp.float32), jnp.ones((8, 128), jnp.float32)
    red, green, blue, clear = lax.fori_loop(0, BLOCKS, add_block, (zero, zero, zero, one))
    opaque = 1.0 - clear
    channels = [0.5 * (opaque + red), green, 0.5 * (opaque - blue), opaque]
    flat = jnp.concatenate([jnp.concatenate([v[0:4], v[4:8]], axis=1) for v in channels], axis=0)
    old = lax.broadcasted_iota(jnp.int32, (256, 256), 0)
    new = lax.broadcasted_iota(jnp.int32, (256, 256), 1)
    spread = jnp.where(new == 2 * lax.rem(old, 128) + lax.div(old, 128), 1.0, 0.0)
    mixed = jnp.dot(flat, spread, precision=lax.Precision.HIGHEST, preferred_element_type=jnp.float32)
    for ch in range(4):
        for par in range(2):
            for t in range(2):
                n = ch * 4 + par * 2 + t
                frame_out[ch, par : par + 1, t * 256 : t * 256 + 256] = mixed[n : n + 1]

    for i in range(2):
        @pl.when(has_next)
        def _(i=i):
            halo(i, 0, whole)(0).wait_send()

        @pl.when(has_prev)
        def _(i=i):
            halo(i, 1, whole)(0).wait_send()

    all_mixed.wait_send()

    @pl.when(self_part)
    def _():
        wait_parts(BLOCKS - 1).wait_send()

    @pl.when(jnp.logical_not(self_part))
    def _():
        wait_parts(BLOCKS).wait_send()

    store_c.wait()
    store_s.wait()


def shards(species):
    f32 = jnp.float32
    plane = pltpu.VMEM((ROWS, COLS), f32)
    padded = pltpu.VMEM((ROWS + 16, COLS), f32)
    dma = pltpu.SemaphoreType.DMA
    fresh, frame = pl.pallas_call(
        kernel,
        out_shape=(
            jax.ShapeDtypeStruct((2, 1, ROWS, COLS), f32),
            jax.ShapeDtypeStruct((4, 2 * ROWS // SIMS, 2 * COLS // GRP), f32),
        ),
        in_specs=[pl.BlockSpec(memory_space=pl.ANY)],
        out_specs=(pl.BlockSpec(memory_space=pl.ANY), pl.BlockSpec(memory_space=pltpu.VMEM)),
        scratch_shapes=[
            padded, padded, plane, plane, plane, plane,
            plane, plane,
            pltpu.VMEM((ROWS, 128), f32),
            pltpu.VMEM((MEMBERS * SLOT, 128), f32),
            pltpu.VMEM((MEMBERS * SLOT, 128), f32),
            pltpu.VMEM((REGION * PIECE, 128), f32),
            pltpu.VMEM((BLOCKS * PIECE, 128), f32),
            dma((2,)), dma((2,)), dma((2, 2)), dma((2, 2, CHUNKS)),
            dma, dma, dma, dma, dma, dma,
        ],
        compiler_params=pltpu.CompilerParams(
            collective_id=0, has_side_effects=True, vmem_limit_bytes=32 * 1024 * 1024
        ),
        cost_estimate=pl.CostEstimate(flops=20_000_000, bytes_accessed=4_000_000, transcendentals=2_000_000),
    )(species)
    return fresh, frame


def solution(mesh):
    return jax.shard_map(
        shards,
        mesh=mesh,
        in_specs=(P(None, ("sim", "grp"), None, None),),
        out_specs=(P(None, ("sim", "grp"), None, None), P(None, "sim", "grp")),
        check_vma=False,
    )
```

time: 220 us -> 75.2 us (0.34)
  waiting for transfers between devices: 91.2 us -> 0 us
  Pallas kernels: 0 us -> 70.6 us
  starting transfers between devices: 52.5 us -> 0 us
  other arithmetic: 41.1 us -> 0 us
  local copies, waits for them, and re-layouts: 30.9 us -> 2.8 us
    pallas_call x0 -> x1, Pallas kernels: none -> 70.6 us  [shards(): pl.pallas_call(kernel, out_shape=(jax.ShapeDtypeStruct((2, 1, ROWS, COLS)...]
    ppermute x9 -> x0, waiting for transfers between devices: 67.3 us -> none  [the longest x7 40.5 us: swapped(): lax.ppermute(value, axis, [(i, i ^ 1 << apart) for i in range(lax.axis_si...]
    ppermute x9 -> x0, starting transfers between devices: 48.9 us -> none  [the longest x7 41.1 us: swapped(): lax.ppermute(value, axis, [(i, i ^ 1 << apart) for i in range(lax.axis_si...]
    all_to_all x1 -> x0, waiting for transfers between devices: 23.9 us -> none  [shards(): lax.all_to_all(samples, 'grp', split_axis=2, concat_axis=0, tiled=True)]
    mul x6 -> x0, other arithmetic: 13.5 us -> none  [the longest x2 9.63 us: shade(): opacity * green_part]
    add x12 -> x0, other arithmetic: 11.7 us -> none  [the longest x9 6.94 us: over(): return front_part + (1.0 - front_part[..., 3:4, :, :]) * back_part]
    sub x12 -> x0, other arithmetic: 9.33 us -> none  [the longest x10 8.22 us: over(): return front_part + (1.0 - front_part[..., 3:4, :, :]) * back_part]
    another operation x2 -> x0, local copies, waits for them, and re-layouts: 6.77 us -> none  [refine(): paired = jnp.stack([even_part, odd_part], axis=axis_num + 1)]
  transfers between devices with their start and end apart: 10 -> 0, of which waited for: 10 -> 0; matrix products, arithmetic and copies ran while one was open for 1% -> 0% of each run, Pallas kernels for 0% -> 0%
where the time goes in v1:
time: 75.2 us; the launch traced here: 74.1 us
  Pallas kernels  70.6 us (94%)
  local copies, waits for them, and re-layouts  2.8 us (4%)
    pallas_call x1, Pallas kernels, shards(): pl.pallas_call(kernel, out_shape=(jax.ShapeDtypeStruct((2, 1, ROWS, COLS)...  70.6 us
    unnamed x4, local copies, waits for them, and re-layouts  2.8 us

profile of v1, /device:TPU:1, one launch (start us, length us, event | category | flops | bytes accessed | tf_op | source)
XLA Modules:
  0.0 74.1 jit_solution(16469304312240616774)
XLA Ops:
  0.6 0.0 copy-start
  0.6 1.2 %copy-done = f32[2,1,128,1024]{3,2,1,0:T(8,128)S(1)} copy-done((f32[2,1,128,1024]{3,2,1,0:T(8,128)S(1)}, f32[2,1,128,1024]{3,2,1,0:T(8,128)}, u32[]{:S(2)}) %copy-start) | copy-done | bytes 1048600
  1.9 70.6 %shard_map.30 = (f32[2,1,128,1024]{3,2,1,0:T(8,128)S(1)}, f32[4,2,512]{2,1,0:T(2,128)S(1)}) custom-call(f32[2,1,128,1024]{3,2,1,0:T(8,128)S(1)} %copy-done), custom_call_target="tpu_custom_call" | custom-call | flops 20000000 | bytes 4000000 | tf_op jit(solution)/shard_map/pallas_call | solution.py:418
  72.5 1.0 %copy.5 = f32[2,1,128,1024]{3,2,1,0:T(8,128)} copy(f32[2,1,128,1024]{3,2,1,0:T(8,128)S(1)} %get-tuple-element.4) | data formatting | bytes 2097152
  73.5 0.6 copy.6
Async XLA Ops:
  0.6 1.2 %copy-start = (f32[2,1,128,1024]{3,2,1,0:T(8,128)S(1)}, f32[2,1,128,1024]{3,2,1,0:T(8,128)}, u32[]{:S(2)}) copy-start(f32[2,1,128,1024]{3,2,1,0:T(8,128)} %species.1) | copy-start | bytes 3145732

commit v2 on v1

--- a/solution.py
+++ b/solution.py
@@ -1,3 +1,5 @@
+import math
+
 import jax
 import jax.numpy as jnp
 from jax import lax
@@ -19,6 +21,8 @@
 CHUNK = ROWS // CHUNKS
 SLOT = 40
 PIECE = 32
+TEAM = MEMBERS // 4
+TOTALS = 64 * 8
 
 DIFF_S, DIFF_C, FEED, KILL = 0.16, 0.08, 0.035, 0.065
 
@@ -40,7 +44,7 @@
 
 def kernel(
     species, next_out, frame_out,
-    sbuf, cbuf, s_up, s_dn, c_up, c_dn, s_new, c_new, edge_cols, sendbuf, recvbuf, pack, parts,
+    sbuf, cbuf, s_up, s_dn, c_up, c_dn, s_new, c_new, edge_cols, sendbuf, recvbuf, totals, pack, parts,
     load_sem, store_sem, halo_send, halo_recv, own_sem, mix_send, mix_recv, part_own, part_send, part_recv,
 ):
     sim, grp = lax.axis_index("sim"), lax.axis_index("grp")
@@ -55,7 +59,13 @@
     def member_of(q, turn):
         return 2 * lax.rem(lax.div(q, 2) + turn, 4) + lax.rem(q, 2)
 
+    def first_chunk(sim):
+        block = lax.div(sim, SUB)
+        place = lax.div(lax.rem(sim, SUB), 2) + 1 + 8 - lax.div(block, 4) - lax.rem(block, 4)
+        return 2 * lax.rem(place, 4)
+
     region = region_of(member, turn)
+    team = lax.div(member, 2)
 
     def source(b):
         t = lax.div(b, 4) + lax.rem(b, 4)
@@ -135,25 +145,79 @@
 
     whole = pl.ds(0, ROWS)
 
-    def send_catalyst(k, _):
+    first_next, first_prev = first_chunk(nxt["sim"]), first_chunk(prev["sim"])
+
+    def send_catalyst(n, _):
         @pl.when(has_next)
         def _():
+            k = lax.rem(first_next + n, CHUNKS)
             halo(1, 0, chunk_rows(k))(k).start()
 
         @pl.when(has_prev)
         def _():
+            k = lax.rem(first_prev + n, CHUNKS)
             halo(1, 1, chunk_rows(k))(k).start()
 
         return 0
 
     lax.fori_loop(0, CHUNKS, send_catalyst, 0)
     loads[1].wait()
-
     loads[0].wait()
+
     lane = lax.broadcasted_iota(jnp.int32, (8, 128), 1)
+    row = lax.broadcasted_iota(jnp.int32, (8, 128), 0)
     beside = [(0, 0), (2, 0), (1, 127), (4, 0), (3, 127), (6, 0), (5, 127), (7, 127)]
 
-    def catalyst_chunk(k, _):
+    def mix(k, x, start, length):
+        m = member_of(k, turn)
+        source_rows = pl.ds(pl.multiple_of((k * GRP + x) * SLOT + start, 8), length)
+        target_rows = pl.ds(pl.multiple_of(seat * SLOT + start, 8), length)
+        away = pltpu.make_async_remote_copy(
+            src_ref=sendbuf.at[source_rows, :],
+            dst_ref=recvbuf.at[target_rows, :],
+            send_sem=mix_send,
+            recv_sem=mix_recv.at[team],
+            device_id=to(block * SUB + m, x),
+            device_id_type=MESH,
+        )
+        here = pltpu.make_async_copy(sendbuf.at[source_rows, :], recvbuf.at[target_rows, :], own_sem)
+        return away, here, m * GRP + x == seat
+
+    def send_tiles(k, start, length):
+        for dx in range(1, GRP + 1):
+            away, here, stays = mix(k, lax.rem(grp + dx, GRP), start, length)
+
+            @pl.when(stays)
+            def _(here=here):
+                here.start()
+
+            @pl.when(jnp.logical_not(stays))
+            def _(away=away):
+                away.start()
+
+    def send_rim(k):
+        top = c_new[pl.ds(pl.multiple_of(jnp.maximum(k * REGION - 8, 0), 8), 8), :]
+        bottom = c_new[pl.ds(pl.multiple_of(jnp.minimum(k * REGION + REGION, ROWS - 8), 8), 8), :]
+        above = jnp.where(k == 0, top[0:1], top[7:8])
+        below = jnp.where(k == SUB - 1, bottom[7:8], bottom[0:1])
+        window = edge_cols[pl.ds(pl.multiple_of(k * REGION, 8), 32), :]
+        window = jnp.concatenate([window, jnp.zeros((96, 128), jnp.float32)], axis=0)
+        cols = pltpu.roll(jnp.transpose(window)[0:8], 121, 1)
+        for x in range(GRP):
+            c = 2 * x * 128
+            tile = pltpu.roll(cols, (4 - 2 * x) % 8, 0)
+            tile = jnp.where(row == 0, above[:, c : c + 128], tile)
+            tile = jnp.where(row == 1, above[:, c + 128 : c + 256], tile)
+            tile = jnp.where(row == 2, below[:, c : c + 128], tile)
+            tile = jnp.where(row == 3, below[:, c + 128 : c + 256], tile)
+            sendbuf[pl.ds(pl.multiple_of((k * GRP + x) * SLOT + 32, 8), 8), :] = tile
+        send_tiles(k, 32, 8)
+
+    first = first_chunk(sim)
+
+    def catalyst_chunk(n, _):
+        k = lax.rem(first + n, CHUNKS)
+
         @pl.when(has_prev)
         def _():
             halo(1, 0, chunk_rows(k))(k).wait_recv()
@@ -169,136 +233,144 @@
             new = c + DIFF_C * lap + s * c * c - (FEED + KILL) * c
             c_new[pl.ds(r, 8), :] = new
             columns = jnp.zeros((8, 128), jnp.float32)
-            for n, (tile, at) in enumerate(beside):
-                moved = pltpu.roll(new[:, tile * 128 : tile * 128 + 128], (n - at) % 128, 1)
-                columns = jnp.where(lane == n, moved, columns)
-            edge_cols[pl.ds(r, 8), :] = columns
+            for i, (tile, at) in enumerate(beside):
+                moved = pltpu.roll(new[:, tile * 128 : tile * 128 + 128], (i - at) % 128, 1)
+                columns = jnp.where(lane == i, moved, columns)
+            edge_cols[pl.ds(pl.multiple_of(r + 8, 8), 8), :] = columns
+            if h == 0:
+                @pl.when(k == 0)
+                def _(columns=columns):
+                    edge_cols[0:8, :] = jnp.broadcast_to(columns[0:1], (8, 128))
+            else:
+                @pl.when(k == CHUNKS - 1)
+                def _(columns=columns):
+                    edge_cols[ROWS + 8 : ROWS + 16, :] = jnp.broadcast_to(columns[7:8], (8, 128))
             for tile in range(COLS // 128):
                 slot = (k * GRP + tile // 2) * SLOT + (h * 2 + tile % 2) * 8
                 sendbuf[pl.ds(pl.multiple_of(slot, 8), 8), :] = new[:, tile * 128 : tile * 128 + 128]
+
+        send_tiles(k, 0, 32)
+
+        @pl.when(n >= 2)
+        def _():
+            send_rim(lax.rem(first + n - 1, CHUNKS))
+
         return 0
 
     lax.fori_loop(0, CHUNKS, catalyst_chunk, 0)
+    last_rims = lambda n, _: (send_rim(lax.rem(first + CHUNKS - 1 + n, CHUNKS)), 0)[1]
+    lax.fori_loop(0, 2, last_rims, 0)
 
     store_c = pltpu.make_async_copy(c_new, next_out.at[1, 0], store_sem.at[1])
     store_c.start()
 
-    beside_t = jnp.transpose(edge_cols[...])[0:8]
-
-    for q in range(SUB):
-        above, below = max(q * REGION - 1, 0), min(q * REGION + REGION, ROWS - 1)
-        cols = pltpu.roll(beside_t, (1 - q * REGION) % ROWS, 1)
-        if q == 0:
-            cols = jnp.where(lane == 0, beside_t, cols)
-        if q == SUB - 1:
-            cols = jnp.where(lane == REGION + 1, pltpu.roll(beside_t, REGION + 2, 1), cols)
-        for x in range(GRP):
-            base = (q * GRP + x) * SLOT + 32
-            for t in range(2):
-                col = (2 * x + t) * 128
-                sendbuf[base + t : base + t + 1, :] = c_new[above : above + 1, col : col + 128]
-                sendbuf[base + 2 + t : base + 3 + t, :] = c_new[below : below + 1, col : col + 128]
-            sendbuf[base + 4 : base + 6, :] = cols[2 * x : 2 * x + 2]
-            sendbuf[base + 6 : base + 8, :] = jnp.zeros((2, 128), jnp.float32)
-
-    def slot_rows(n):
-        return pl.ds(pl.multiple_of(n * SLOT, SLOT), SLOT)
-
-    def mix(other):
-        m, x = lax.div(other, GRP), lax.rem(other, GRP)
+    @pl.when(has_next)
+    def _():
+        halo(0, 0, whole)(0).start()
+
+    @pl.when(has_prev)
+    def _():
+        halo(0, 1, whole)(0).start()
+
+    def wait_mixed(count, t):
+        some = pl.ds(0, count * SLOT)
         return pltpu.make_async_remote_copy(
-            src_ref=sendbuf.at[slot_rows(region_of(m, turn) * GRP + x), :],
-            dst_ref=recvbuf.at[slot_rows(seat), :],
-            send_sem=mix_send,
-            recv_sem=mix_recv,
-            device_id=to(block * SUB + m, x),
-            device_id_type=MESH,
-        )
-
-    def send_region(d, _):
-        mix(lax.rem(seat + d, MEMBERS)).start()
-        return 0
-
-    lax.fori_loop(1, MEMBERS, send_region, 0)
-    own = pltpu.make_async_copy(
-        sendbuf.at[slot_rows(region * GRP + grp), :], recvbuf.at[slot_rows(seat), :], own_sem
-    )
-    own.start()
-
-    @pl.when(has_next)
-    def _():
-        halo(0, 0, whole)(0).start()
-
-    @pl.when(has_prev)
-    def _():
-        halo(0, 1, whole)(0).start()
-
-    own.wait()
-    others = pl.ds(0, (MEMBERS - 1) * SLOT)
-    all_mixed = pltpu.make_async_remote_copy(
-        src_ref=sendbuf.at[others, :], dst_ref=recvbuf.at[others, :],
-        send_sem=mix_send, recv_sem=mix_recv, device_id=to(sim, grp), device_id_type=MESH,
-    )
-    all_mixed.wait_recv()
-
-    sides = jnp.concatenate(
-        [
-            recvbuf[pl.ds(36, MEMBERS, stride=SLOT), :],
-            recvbuf[pl.ds(37, MEMBERS, stride=SLOT), :],
-            jnp.zeros((128 - 2 * MEMBERS, 128), jnp.float32),
-        ],
-        axis=0,
-    )
-    sides = jnp.transpose(sides)
-    row = lax.broadcasted_iota(jnp.int32, (8, 128), 0)
+            src_ref=sendbuf.at[some, :], dst_ref=recvbuf.at[some, :],
+            send_sem=mix_send, recv_sem=mix_recv.at[t], device_id=to(sim, grp), device_id_type=MESH,
+        )
+
     extinct = 6.0 / (BLOCKS * MEMBERS)
+    log2e = math.log2(math.e)
+    thin, narrow = -extinct * log2e / 256.0, -8.0 * log2e / 256.0
+
+    def render(i, _):
+        t_now = lax.rem(team + 6 - i, 4)
+
+        @pl.when(t_now == team)
+        def _():
+            one_slot = pl.ds(0, SLOT)
+            pltpu.make_async_copy(sendbuf.at[one_slot, :], recvbuf.at[one_slot, :], own_sem).wait()
+            wait_mixed(TEAM - 1, team).wait_recv()
+
+        @pl.when(t_now != team)
+        def _():
+            wait_mixed(TEAM, t_now).wait_recv()
+
+        base = t_now * (TEAM * SLOT)
+        sides = jnp.concatenate(
+            [
+                recvbuf[pl.ds(base + 36, TEAM, stride=SLOT), :],
+                recvbuf[pl.ds(base + 37, TEAM, stride=SLOT), :],
+                jnp.zeros((128 - 2 * TEAM, 128), jnp.float32),
+            ],
+            axis=0,
+        )
+        sides = jnp.transpose(sides)
+
+        for h in range(2):
+            for par in range(2):
+                near = 2 * par + 8 * h
+                side = 3.0 * sides[1 + 8 * h : 9 + 8 * h] + sides[near : near + 8]
+
+                def layer(p, sums, h=h, par=par, side=side):
+                    at = pl.multiple_of(base + p * SLOT, 8)
+                    rim = recvbuf[pl.ds(at + 32, 8), :]
+                    rows = []
+                    for t in range(2):
+                        mine = recvbuf[pl.ds(at + (2 * h + t) * 8, 8), :]
+                        across = recvbuf[pl.ds(at + (2 - 2 * h + t) * 8, 8), :]
+                        if par == 0:
+                            beyond = rim[t : t + 1] if h == 0 else across[7:8]
+                            shifted = jnp.where(row == 0, beyond, pltpu.roll(mine, 1, 0))
+                        else:
+                            beyond = rim[2 + t : 3 + t] if h == 1 else across[0:1]
+                            shifted = jnp.where(row == 7, beyond, pltpu.roll(mine, 7, 0))
+                        rows.append(3.0 * mine + shifted)
+                    leftmost = pltpu.roll(side, lax.rem(128 - p, 128), 1)
+                    rightmost = pltpu.roll(side, 127 - TEAM - p, 1)
+                    fwd = [pltpu.roll(v, 1, 1) for v in rows]
+                    bwd = [pltpu.roll(v, 127, 1) for v in rows]
+                    low = [jnp.where(lane == 0, leftmost, fwd[0]), jnp.where(lane == 0, fwd[0], fwd[1])]
+                    high = [jnp.where(lane == 127, bwd[1], bwd[0]), jnp.where(lane == 127, rightmost, bwd[1])]
+                    result = []
+                    for cpar in range(2):
+                        for t in range(2):
+                            q = 3.0 * rows[t] + (low, high)[cpar][t]
+                            red, green, blue, clear = sums[(cpar * 2 + t) * 4 : (cpar * 2 + t) * 4 + 4]
+                            after = clear * jnp.exp2((q * q) * thin)
+                            weight = clear - after
+                            mid = q - 8.0
+                            warm = mid * (3.0 / 16.0)
+                            red = red + weight * jnp.tanh(warm)
+                            green = green + weight * jnp.exp2((mid * mid) * narrow)
+                            blue = blue + weight * jnp.tanh(warm + 0.6)
+                            result += [red, green, blue, after]
+                    return tuple(result)
+
+                zero, one = jnp.zeros((8, 128), jnp.float32), jnp.ones((8, 128), jnp.float32)
+                sums = lax.fori_loop(0, TEAM, layer, (zero, zero, zero, one) * 4, unroll=True)
+                for j in range(16):
+                    at = t_now * TOTALS + ((h * 2 + par) * 16 + j) * 8
+                    totals[pl.ds(pl.multiple_of(at, 8), 8), :] = sums[j]
+        return 0
+
+    lax.fori_loop(0, 4, render, 0)
 
     for h in range(2):
         for par in range(2):
-            near = 2 * par
-            side = 0.75 * sides[1 + 8 * h : 9 + 8 * h] + 0.25 * sides[near + 8 * h : near + 8 * h + 8]
-
-            def layer(p, totals, h=h, par=par, side=side):
-                base = pl.multiple_of(p * SLOT, 8)
-                rim = recvbuf[pl.ds(base + 32, 8), :]
-                rows = []
-                for t in range(2):
-                    mine = recvbuf[pl.ds(base + (2 * h + t) * 8, 8), :]
-                    across = recvbuf[pl.ds(base + (2 - 2 * h + t) * 8, 8), :]
-                    if par == 0:
-                        beyond = rim[t : t + 1] if h == 0 else across[7:8]
-                        shifted = jnp.where(row == 0, beyond, pltpu.roll(mine, 1, 0))
-                    else:
-                        beyond = rim[2 + t : 3 + t] if h == 1 else across[0:1]
-                        shifted = jnp.where(row == 7, beyond, pltpu.roll(mine, 7, 0))
-                    rows.append(0.75 * mine + 0.25 * shifted)
-                leftmost = pltpu.roll(side, lax.rem(128 - p, 128), 1)
-                rightmost = pltpu.roll(side, 127 - MEMBERS - p, 1)
-                fwd = [pltpu.roll(v, 1, 1) for v in rows]
-                bwd = [pltpu.roll(v, 127, 1) for v in rows]
-                low = [jnp.where(lane == 0, leftmost, fwd[0]), jnp.where(lane == 0, fwd[0], fwd[1])]
-                high = [jnp.where(lane == 127, bwd[1], bwd[0]), jnp.where(lane == 127, rightmost, bwd[1])]
-                result = []
-                for cpar in range(2):
-                    for t in range(2):
-                        q = 0.75 * rows[t] + 0.25 * (low, high)[cpar][t]
-                        red, green, blue, clear = totals[(cpar * 2 + t) * 4 : (cpar * 2 + t) * 4 + 4]
-                        after = clear * jnp.exp(-extinct * (q * q))
-                        weight = clear - after
-                        mid = q - 0.5
-                        red = red + weight * jnp.tanh(3.0 * mid)
-                        green = green + weight * jnp.exp(-8.0 * (mid * mid))
-                        blue = blue + weight * jnp.tanh(3.0 * (q - 0.3))
-                        result += [red, green, blue, after]
-                return tuple(result)
-
-            zero, one = jnp.zeros((8, 128), jnp.float32), jnp.ones((8, 128), jnp.float32)
-            totals = lax.fori_loop(0, MEMBERS, layer, (zero, zero, zero, one) * 4)
             for cpar in range(2):
                 for t in range(2):
-                    for ch in range(4):
+                    base = ((h * 2 + par) * 16 + (cpar * 2 + t) * 4) * 8
+                    got = [[totals[i * TOTALS + base + 8 * ch : i * TOTALS + base + 8 * ch + 8, :] for ch in range(4)] for i in range(4)]
+                    red, green, blue, clear = got[0]
+                    for i in range(1, 4):
+                        red = red + clear * got[i][0]
+                        green = green + clear * got[i][1]
+                        blue = blue + clear * got[i][2]
+                        clear = clear * got[i][3]
+                    for ch, value in enumerate((red, green, blue, clear)):
                         at = 8 * h * PIECE + ch * 8 + cpar * 4 + par * 2 + t
-                        pack[pl.ds(at, 8, stride=PIECE), :] = totals[(cpar * 2 + t) * 4 + ch]
+                        pack[pl.ds(at, 8, stride=PIECE), :] = value
 
     def piece_rows(n):
         return pl.ds(pl.multiple_of(n * PIECE, PIECE), PIECE)
@@ -345,7 +417,7 @@
         s_new[pl.ds(r, 8), :] = s + DIFF_S * lap - s * c * c + FEED * (1.0 - s)
         return 0
 
-    lax.fori_loop(0, ROWS // 8, substrate_rows, 0)
+    lax.fori_loop(0, ROWS // 8, substrate_rows, 0, unroll=4)
     store_s = pltpu.make_async_copy(s_new, next_out.at[0, 0], store_sem.at[0])
     store_s.start()
 
@@ -373,7 +445,7 @@
         )
 
     zero, one = jnp.zeros((8, 128), jnp.float32), jnp.ones((8, 128), jnp.float32)
-    red, green, blue, clear = lax.fori_loop(0, BLOCKS, add_block, (zero, zero, zero, one))
+    red, green, blue, clear = lax.fori_loop(0, BLOCKS, add_block, (zero, zero, zero, one), unroll=True)
     opaque = 1.0 - clear
     channels = [0.5 * (opaque + red), green, 0.5 * (opaque - blue), opaque]
     flat = jnp.concatenate([jnp.concatenate([v[0:4], v[4:8]], axis=1) for v in channels], axis=0)
@@ -396,7 +468,7 @@
         def _(i=i):
             halo(i, 1, whole)(0).wait_send()
 
-    all_mixed.wait_send()
+    wait_mixed(MEMBERS - 1, team).wait_send()
 
     @pl.when(self_part)
     def _():
@@ -421,18 +493,19 @@
             jax.ShapeDtypeStruct((2, 1, ROWS, COLS), f32),
             jax.ShapeDtypeStruct((4, 2 * ROWS // SIMS, 2 * COLS // GRP), f32),
         ),
-        in_specs=[pl.BlockSpec(memory_space=pl.ANY)],
+        in_specs=[pl.BlockSpec(memory_space=pltpu.HBM)],
         out_specs=(pl.BlockSpec(memory_space=pl.ANY), pl.BlockSpec(memory_space=pltpu.VMEM)),
         scratch_shapes=[
             padded, padded, plane, plane, plane, plane,
             plane, plane,
-            pltpu.VMEM((ROWS, 128), f32),
+            pltpu.VMEM((ROWS + 16, 128), f32),
             pltpu.VMEM((MEMBERS * SLOT, 128), f32),
             pltpu.VMEM((MEMBERS * SLOT, 128), f32),
+            pltpu.VMEM((4 * TOTALS, 128), f32),
             pltpu.VMEM((REGION * PIECE, 128), f32),
             pltpu.VMEM((BLOCKS * PIECE, 128), f32),
             dma((2,)), dma((2,)), dma((2, 2)), dma((2, 2, CHUNKS)),
-            dma, dma, dma, dma, dma, dma,
+            dma, dma, dma((4,)), dma, dma, dma,
         ],
         compiler_params=pltpu.CompilerParams(
             collective_id=0, has_side_effects=True, vmem_limit_bytes=32 * 1024 * 1024

time: 75.2 us -> 60.6 us (0.81)
  the two profiles are of different devices: /device:TPU:1 before, /device:TPU:217 now
where the time goes in v2:
time: 60.6 us; the launch traced here: 60.4 us
  Pallas kernels  57 us (94%)
  local copies, waits for them, and re-layouts  2.8 us (5%)
  between operations  0.65 us (1%)
    pallas_call x1, Pallas kernels, shards(): pl.pallas_call(kernel, out_shape=(jax.ShapeDtypeStruct((2, 1, ROWS, COLS)...  57 us
    unnamed x4, local copies, waits for them, and re-layouts  2.8 us

profile of v2, /device:TPU:217, one launch (start us, length us, event | category | flops | bytes accessed | tf_op | source)
XLA Modules:
  0.0 60.4 jit_solution(3245575177885835355)
XLA Ops:
  0.6 0.0 copy-start
  0.6 1.2 %copy-done = f32[2,1,128,1024]{3,2,1,0:T(8,128)S(1)} copy-done((f32[2,1,128,1024]{3,2,1,0:T(8,128)S(1)}, f32[2,1,128,1024]{3,2,1,0:T(8,128)}, u32[]{:S(2)}) %copy-start) | copy-done | bytes 1048600
  1.9 57.0 %shard_map.30 = (f32[2,1,128,1024]{3,2,1,0:T(8,128)S(1)}, f32[4,2,512]{2,1,0:T(2,128)S(1)}) custom-call(f32[2,1,128,1024]{3,2,1,0:T(8,128)S(1)} %copy-done), custom_call_target="tpu_custom_call" | custom-call | flops 20000000 | bytes 4000000 | tf_op jit(solution)/shard_map/pallas_call | solution.py:490
  58.9 1.0 %copy.5 = f32[2,1,128,1024]{3,2,1,0:T(8,128)} copy(f32[2,1,128,1024]{3,2,1,0:T(8,128)S(1)} %get-tuple-element.4) | data formatting | bytes 2097152
  59.8 0.6 %copy.6 = f32[4,2,512]{2,1,0:T(2,128)} copy(f32[4,2,512]{2,1,0:T(2,128)S(1)} %get-tuple-element.5) | data formatting | bytes 32768
Async XLA Ops:
  0.6 1.2 %copy-start = (f32[2,1,128,1024]{3,2,1,0:T(8,128)S(1)}, f32[2,1,128,1024]{3,2,1,0:T(8,128)}, u32[]{:S(2)}) copy-start(f32[2,1,128,1024]{3,2,1,0:T(8,128)} %species.1) | copy-start | bytes 3145732

commit v3 on v2

--- a/solution.py
+++ b/solution.py
@@ -44,8 +44,8 @@
 
 def kernel(
     species, next_out, frame_out,
-    sbuf, cbuf, s_up, s_dn, c_up, c_dn, s_new, c_new, edge_cols, sendbuf, recvbuf, totals, pack, parts,
-    load_sem, store_sem, halo_send, halo_recv, own_sem, mix_send, mix_recv, part_own, part_send, part_recv,
+    sbuf, cbuf, s_up, s_dn, c_up, c_dn, rs_up, rs_dn, rc_up, rc_dn, s_new, c_new, edge_cols, sendbuf, recvbuf, totals, pack, parts,
+    load_sem, store_sem, halo_send, halo_recv, relay_send, relay_recv, own_sem, mix_send, mix_recv, part_own, part_send, part_recv,
 ):
     sim, grp = lax.axis_index("sim"), lax.axis_index("grp")
     plane = sim * GRP + grp
@@ -81,15 +81,26 @@
     has_prev, has_next = plane > 0, plane < SIMS * GRP - 1
     prev = to(lax.div(plane - 1, GRP), lax.rem(plane - 1 + GRP, GRP))
     nxt = to(lax.div(plane + 1, GRP), lax.rem(plane + 1, GRP))
+
+    odd = lax.rem(sim, 2)
+    sim_a = sim + odd - 1
+    sim_b = sim_a + 1
+    edge = ((grp == 0) | (grp == GRP - 1)) & (sim_a >= 0) & (sim_b < SIMS)
+    is_a = edge & (odd == 1) & (grp == GRP - 1)
+    is_b = edge & (odd == 0) & (grp == 0)
+    is_relay = edge & jnp.logical_not(is_a | is_b)
+    relays = (to(sim_a, 0), to(sim_b, GRP - 1))
+    ends = (to(sim_b, 0), to(sim_a, GRP - 1))
+    my_half = lax.div(grp, GRP - 1)
+    straight_next = has_next & jnp.logical_not(is_a)
+    straight_prev = has_prev & jnp.logical_not(is_b)
     barrier = pltpu.get_barrier_semaphore()
-
-    @pl.when(has_prev)
-    def _():
-        pl.semaphore_signal(barrier, inc=1, device_id=prev, device_id_type=MESH)
-
-    @pl.when(has_next)
-    def _():
-        pl.semaphore_signal(barrier, inc=1, device_id=nxt, device_id_type=MESH)
+    for wanted, other in (
+        (straight_prev, prev), (straight_next, nxt), (edge, to(sim_a + sim_b - sim, grp)),
+    ):
+        @pl.when(wanted)
+        def _(other=other):
+            pl.semaphore_signal(barrier, inc=1, device_id=other, device_id_type=MESH)
 
     def greet_member(d, _):
         other = lax.rem(seat + d, MEMBERS)
@@ -126,41 +137,88 @@
 
     self_part = lax.div(sim, REGION) == region
     expected = MEMBERS - 1 + BLOCKS - self_part.astype(jnp.int32)
-    expected = expected + has_prev.astype(jnp.int32) + has_next.astype(jnp.int32)
+    for wanted in (straight_prev, straight_next, edge):
+        expected = expected + wanted.astype(jnp.int32)
     pl.semaphore_wait(barrier, expected)
 
+    targets, passing = ((s_up, s_dn), (c_up, c_dn)), ((rs_up, rs_dn), (rc_up, rc_dn))
+
     def halo(i, way, rows):
-        target = ((s_up, s_dn), (c_up, c_dn))[i][way]
         return lambda chunk: pltpu.make_async_remote_copy(
             src_ref=species.at[i, 0, rows, :],
-            dst_ref=target.at[rows, :],
+            dst_ref=targets[i][way].at[rows, :],
             send_sem=halo_send.at[i, way],
             recv_sem=halo_recv.at[i, way, chunk],
             device_id=(nxt, prev)[way],
             device_id_type=MESH,
         )
 
+    def to_relay(i, way, rows, there, chunk, half):
+        return pltpu.make_async_remote_copy(
+            src_ref=species.at[i, 0, rows, :],
+            dst_ref=passing[i][way].at[there, :],
+            send_sem=halo_send.at[i, way],
+            recv_sem=relay_recv.at[i, way, chunk],
+            device_id=relays[half],
+            device_id_type=MESH,
+        )
+
+    def from_relay(i, way, rows, there, chunk):
+        return pltpu.make_async_remote_copy(
+            src_ref=passing[i][way].at[rows, :],
+            dst_ref=targets[i][way].at[there, :],
+            send_sem=relay_send.at[i, way],
+            recv_sem=halo_recv.at[i, way, chunk],
+            device_id=ends[way],
+            device_id_type=MESH,
+        )
+
     def chunk_rows(k):
         return pl.ds(pl.multiple_of(k * CHUNK, CHUNK), CHUNK)
 
+    def half_chunk(k, half):
+        return pl.ds(pl.multiple_of(k * CHUNK + half * 8, 8), 8)
+
+    def relay_rows(k):
+        return pl.ds(pl.multiple_of(k * 8, 8), 8)
+
     whole = pl.ds(0, ROWS)
-
-    first_next, first_prev = first_chunk(nxt["sim"]), first_chunk(prev["sim"])
+    half_rows = (pl.ds(0, ROWS // 2), pl.ds(ROWS // 2, ROWS // 2))
+    firsts = (first_chunk(nxt["sim"]), first_chunk(prev["sim"]))
 
     def send_catalyst(n, _):
-        @pl.when(has_next)
-        def _():
-            k = lax.rem(first_next + n, CHUNKS)
-            halo(1, 0, chunk_rows(k))(k).start()
-
-        @pl.when(has_prev)
-        def _():
-            k = lax.rem(first_prev + n, CHUNKS)
-            halo(1, 1, chunk_rows(k))(k).start()
+        for way, straight, end in ((0, straight_next, is_a), (1, straight_prev, is_b)):
+            k = lax.rem(firsts[way] + n, CHUNKS)
+
+            @pl.when(straight)
+            def _(way=way, k=k):
+                halo(1, way, chunk_rows(k))(k).start()
+
+            @pl.when(end)
+            def _(way=way, k=k):
+                for half in range(2):
+                    to_relay(1, way, half_chunk(k, half), relay_rows(k), k, half).start()
 
         return 0
 
-    lax.fori_loop(0, CHUNKS, send_catalyst, 0)
+    def pass_catalyst(n):
+        for way in range(2):
+            k = lax.rem(first_chunk((sim_b, sim_a)[way]) + n, CHUNKS)
+            to_relay(1, way, half_chunk(k, 0), relay_rows(k), k, 0).wait_recv()
+            from_relay(1, way, relay_rows(k), half_chunk(k, my_half), k).start()
+
+    ahead = CHUNKS // 2
+    lax.fori_loop(0, ahead, send_catalyst, 0)
+
+    def send_substrate(early):
+        for way, end in ((0, is_a), (1, is_b)):
+            half = 1 - way if early else way
+
+            @pl.when(end)
+            def _(way=way, half=half):
+                to_relay(0, way, half_rows[half], half_rows[0], 0, half).start()
+
+    send_substrate(True)
     loads[1].wait()
     loads[0].wait()
 
@@ -217,6 +275,14 @@
 
     def catalyst_chunk(n, _):
         k = lax.rem(first + n, CHUNKS)
+
+        @pl.when(n < CHUNKS - ahead)
+        def _():
+            send_catalyst(n + ahead, 0)
+
+        @pl.when(is_relay)
+        def _():
+            pass_catalyst(n)
 
         @pl.when(has_prev)
         def _():
@@ -264,13 +330,15 @@
     store_c = pltpu.make_async_copy(c_new, next_out.at[1, 0], store_sem.at[1])
     store_c.start()
 
-    @pl.when(has_next)
+    @pl.when(straight_next)
     def _():
         halo(0, 0, whole)(0).start()
 
-    @pl.when(has_prev)
+    @pl.when(straight_prev)
     def _():
         halo(0, 1, whole)(0).start()
+
+    send_substrate(False)
 
     def wait_mixed(count, t):
         some = pl.ds(0, count * SLOT)
@@ -402,6 +470,13 @@
         mine.start()
         mine.wait()
 
+    @pl.when(is_relay)
+    def _():
+        for way in range(2):
+            to_relay(0, way, half_rows[0], half_rows[0], 0, 0).wait_recv()
+            there = pl.ds(pl.multiple_of(my_half * (ROWS // 2), 8), ROWS // 2)
+            from_relay(0, way, half_rows[0], there, 0).start()
+
     @pl.when(has_prev)
     def _():
         halo(0, 0, whole)(0).wait_recv()
@@ -468,6 +543,12 @@
         def _(i=i):
             halo(i, 1, whole)(0).wait_send()
 
+    @pl.when(is_relay)
+    def _():
+        for i in range(2):
+            for way in range(2):
+                from_relay(i, way, half_rows[0], half_rows[0], 0).wait_send()
+
     wait_mixed(MEMBERS - 1, team).wait_send()
 
     @pl.when(self_part)
@@ -486,6 +567,7 @@
     f32 = jnp.float32
     plane = pltpu.VMEM((ROWS, COLS), f32)
     padded = pltpu.VMEM((ROWS + 16, COLS), f32)
+    half_plane = pltpu.VMEM((ROWS // 2, COLS), f32)
     dma = pltpu.SemaphoreType.DMA
     fresh, frame = pl.pallas_call(
         kernel,
@@ -497,6 +579,7 @@
         out_specs=(pl.BlockSpec(memory_space=pl.ANY), pl.BlockSpec(memory_space=pltpu.VMEM)),
         scratch_shapes=[
             padded, padded, plane, plane, plane, plane,
+            half_plane, half_plane, half_plane, half_plane,
             plane, plane,
             pltpu.VMEM((ROWS + 16, 128), f32),
             pltpu.VMEM((MEMBERS * SLOT, 128), f32),
@@ -504,14 +587,14 @@
             pltpu.VMEM((4 * TOTALS, 128), f32),
             pltpu.VMEM((REGION * PIECE, 128), f32),
             pltpu.VMEM((BLOCKS * PIECE, 128), f32),
-            dma((2,)), dma((2,)), dma((2, 2)), dma((2, 2, CHUNKS)),
+            dma((2,)), dma((2,)), dma((2, 2)), dma((2, 2, CHUNKS)), dma((2, 2)), dma((2, 2, CHUNKS)),
             dma, dma, dma((4,)), dma, dma, dma,
         ],
         compiler_params=pltpu.CompilerParams(
             collective_id=0, has_side_effects=True, vmem_limit_bytes=32 * 1024 * 1024
         ),
         cost_estimate=pl.CostEstimate(flops=20_000_000, bytes_accessed=4_000_000, transcendentals=2_000_000),
-    )(species)
+    )(pltpu.with_memory_space_constraint(species, pltpu.HBM))
     return fresh, frame
 
 

time: 60.6 us -> 66.3 us (1.094)
  the two profiles are of different devices: /device:TPU:217 before, /device:TPU:8 now
where the time goes in v3:
time: 66.3 us; the launch traced here: 66.2 us
  Pallas kernels  64 us (97%)
  local copies, waits for them, and re-layouts  1.58 us (2%)
    pallas_call x1, Pallas kernels, shards(): pl.pallas_call(kernel, out_shape=(jax.ShapeDtypeStruct((2, 1, ROWS, COLS)...  64 us
    unnamed x2, local copies, waits for them, and re-layouts  1.58 us

profile of v3, /device:TPU:8, one launch (start us, length us, event | category | flops | bytes accessed | tf_op | source)
XLA Modules:
  0.0 66.2 jit_solution(9313940287255671509)
XLA Ops:
  0.6 64.0 %shard_map.30 = (f32[2,1,128,1024]{3,2,1,0:T(8,128)S(1)}, f32[4,2,512]{2,1,0:T(2,128)S(1)}) custom-call(f32[2,1,128,1024]{3,2,1,0:T(8,128)} %species.1), custom_call_target="tpu_custom_call" | custom-call | flops 20000000 | bytes 4000000 | tf_op jit(solution)/shard_map/pallas_call | solution.py:572
  64.6 1.0 %copy.5 = f32[2,1,128,1024]{3,2,1,0:T(8,128)} copy(f32[2,1,128,1024]{3,2,1,0:T(8,128)S(1)} %get-tuple-element.4) | data formatting | bytes 2097152
  65.6 0.6 copy.6

commit v4 on v2

--- a/solution.py
+++ b/solution.py
@@ -31,15 +31,13 @@
     return {"sim": sim, "grp": grp}
 
 
-def laplacian(buf, up, dn, r):
+def in_plane(buf, r):
     window = buf[pl.ds(r, 24), :]
     center = window[8:16]
     lane = lax.broadcasted_iota(jnp.int32, (8, COLS), 1)
     left = jnp.where(lane == 0, 0.0, pltpu.roll(center, 1, 1))
     right = jnp.where(lane == COLS - 1, 0.0, pltpu.roll(center, COLS - 1, 1))
-    total = up[pl.ds(r, 8), :] + dn[pl.ds(r, 8), :]
-    total = total + window[7:15] + window[9:17] + left + right
-    return center, total - 6.0 * center
+    return center, window[7:15] + window[9:17] + left + right - 6.0 * center
 
 
 def kernel(
@@ -163,6 +161,15 @@
     lax.fori_loop(0, CHUNKS, send_catalyst, 0)
     loads[1].wait()
     loads[0].wait()
+
+    def catalyst_rows(i, _):
+        r = pl.multiple_of(8 * i, 8)
+        c, lap = in_plane(cbuf, r)
+        s = sbuf[pl.ds(pl.multiple_of(r + 8, 8), 8), :]
+        c_new[pl.ds(r, 8), :] = c + DIFF_C * lap + s * c * c - (FEED + KILL) * c
+        return 0
+
+    lax.fori_loop(0, ROWS // 8, catalyst_rows, 0, unroll=4)
 
     lane = lax.broadcasted_iota(jnp.int32, (8, 128), 1)
     row = lax.broadcasted_iota(jnp.int32, (8, 128), 0)
@@ -181,28 +188,33 @@
             device_id_type=MESH,
         )
         here = pltpu.make_async_copy(sendbuf.at[source_rows, :], recvbuf.at[target_rows, :], own_sem)
-        return away, here, m * GRP + x == seat
+        return away, here
 
     def send_tiles(k, start, length):
-        for dx in range(1, GRP + 1):
-            away, here, stays = mix(k, lax.rem(grp + dx, GRP), start, length)
-
-            @pl.when(stays)
-            def _(here=here):
-                here.start()
-
-            @pl.when(jnp.logical_not(stays))
-            def _(away=away):
+        copies = [mix(k, lax.rem(grp + dx, GRP), start, length) for dx in range(1, GRP + 1)]
+
+        @pl.when(k != region)
+        def _():
+            for away, _ in copies:
                 away.start()
 
-    def send_rim(k):
+        @pl.when(k == region)
+        def _():
+            for away, _ in copies[:-1]:
+                away.start()
+            copies[-1][1].start()
+
+    def rim(k):
         top = c_new[pl.ds(pl.multiple_of(jnp.maximum(k * REGION - 8, 0), 8), 8), :]
         bottom = c_new[pl.ds(pl.multiple_of(jnp.minimum(k * REGION + REGION, ROWS - 8), 8), 8), :]
         above = jnp.where(k == 0, top[0:1], top[7:8])
         below = jnp.where(k == SUB - 1, bottom[7:8], bottom[0:1])
         window = edge_cols[pl.ds(pl.multiple_of(k * REGION, 8), 32), :]
         window = jnp.concatenate([window, jnp.zeros((96, 128), jnp.float32)], axis=0)
-        cols = pltpu.roll(jnp.transpose(window)[0:8], 121, 1)
+        raw = jnp.transpose(window)[0:8]
+        cols = pltpu.roll(raw, 121, 1)
+        cols = jnp.where((lane == 0) & (k == 0), pltpu.roll(raw, 120, 1), cols)
+        cols = jnp.where((lane == REGION + 1) & (k == SUB - 1), pltpu.roll(raw, 122, 1), cols)
         for x in range(GRP):
             c = 2 * x * 128
             tile = pltpu.roll(cols, (4 - 2 * x) % 8, 0)
@@ -211,12 +223,14 @@
             tile = jnp.where(row == 2, below[:, c : c + 128], tile)
             tile = jnp.where(row == 3, below[:, c + 128 : c + 256], tile)
             sendbuf[pl.ds(pl.multiple_of((k * GRP + x) * SLOT + 32, 8), 8), :] = tile
-        send_tiles(k, 32, 8)
 
     first = first_chunk(sim)
 
+    def chunk_at(n):
+        return lax.rem(first + n, CHUNKS)
+
     def catalyst_chunk(n, _):
-        k = lax.rem(first + n, CHUNKS)
+        k = chunk_at(n)
 
         @pl.when(has_prev)
         def _():
@@ -226,40 +240,34 @@
         def _():
             halo(1, 1, chunk_rows(k))(k).wait_recv()
 
+        rim(chunk_at(n + CHUNKS - 2))
         for h in range(CHUNK // 8):
             r = pl.multiple_of(k * CHUNK + 8 * h, 8)
-            c, lap = laplacian(cbuf, c_up, c_dn, r)
-            s = sbuf[pl.ds(pl.multiple_of(r + 8, 8), 8), :]
-            new = c + DIFF_C * lap + s * c * c - (FEED + KILL) * c
-            c_new[pl.ds(r, 8), :] = new
+            rows = pl.ds(r, 8)
+            new = c_new[rows, :] + DIFF_C * (c_up[rows, :] + c_dn[rows, :])
+            c_new[rows, :] = new
             columns = jnp.zeros((8, 128), jnp.float32)
             for i, (tile, at) in enumerate(beside):
                 moved = pltpu.roll(new[:, tile * 128 : tile * 128 + 128], (i - at) % 128, 1)
                 columns = jnp.where(lane == i, moved, columns)
             edge_cols[pl.ds(pl.multiple_of(r + 8, 8), 8), :] = columns
-            if h == 0:
-                @pl.when(k == 0)
-                def _(columns=columns):
-                    edge_cols[0:8, :] = jnp.broadcast_to(columns[0:1], (8, 128))
-            else:
-                @pl.when(k == CHUNKS - 1)
-                def _(columns=columns):
-                    edge_cols[ROWS + 8 : ROWS + 16, :] = jnp.broadcast_to(columns[7:8], (8, 128))
             for tile in range(COLS // 128):
                 slot = (k * GRP + tile // 2) * SLOT + (h * 2 + tile % 2) * 8
                 sendbuf[pl.ds(pl.multiple_of(slot, 8), 8), :] = new[:, tile * 128 : tile * 128 + 128]
 
         send_tiles(k, 0, 32)
 
-        @pl.when(n >= 2)
-        def _():
-            send_rim(lax.rem(first + n - 1, CHUNKS))
+        @pl.when(n >= 3)
+        def _():
+            send_tiles(chunk_at(n - 2), 32, 8)
 
         return 0
 
     lax.fori_loop(0, CHUNKS, catalyst_chunk, 0)
-    last_rims = lambda n, _: (send_rim(lax.rem(first + CHUNKS - 1 + n, CHUNKS)), 0)[1]
-    lax.fori_loop(0, 2, last_rims, 0)
+    for n in (CHUNKS - 2, CHUNKS - 1, CHUNKS):
+        rim(chunk_at(n))
+    for n in (CHUNKS - 2, CHUNKS - 1, CHUNKS):
+        send_tiles(chunk_at(n), 32, 8)
 
     store_c = pltpu.make_async_copy(c_new, next_out.at[1, 0], store_sem.at[1])
     store_c.start()
@@ -326,7 +334,7 @@
                             beyond = rim[2 + t : 3 + t] if h == 1 else across[0:1]
                             shifted = jnp.where(row == 7, beyond, pltpu.roll(mine, 7, 0))
                         rows.append(3.0 * mine + shifted)
-                    leftmost = pltpu.roll(side, lax.rem(128 - p, 128), 1)
+                    leftmost = pltpu.roll(side, (128 - p) % 128, 1)
                     rightmost = pltpu.roll(side, 127 - TEAM - p, 1)
                     fwd = [pltpu.roll(v, 1, 1) for v in rows]
                     bwd = [pltpu.roll(v, 127, 1) for v in rows]
@@ -348,13 +356,18 @@
                     return tuple(result)
 
                 zero, one = jnp.zeros((8, 128), jnp.float32), jnp.ones((8, 128), jnp.float32)
-                sums = lax.fori_loop(0, TEAM, layer, (zero, zero, zero, one) * 4, unroll=True)
+                sums = (zero, zero, zero, one) * 4
+                for p in range(TEAM):
+                    sums = layer(p, sums)
                 for j in range(16):
                     at = t_now * TOTALS + ((h * 2 + par) * 16 + j) * 8
                     totals[pl.ds(pl.multiple_of(at, 8), 8), :] = sums[j]
         return 0
 
     lax.fori_loop(0, 4, render, 0)
+
+    def piece_rows(n):
+        return pl.ds(pl.multiple_of(n * PIECE, PIECE), PIECE)
 
     for h in range(2):
         for par in range(2):
@@ -372,27 +385,24 @@
                         at = 8 * h * PIECE + ch * 8 + cpar * 4 + par * 2 + t
                         pack[pl.ds(at, 8, stride=PIECE), :] = value
 
-    def piece_rows(n):
-        return pl.ds(pl.multiple_of(n * PIECE, PIECE), PIECE)
-
-    def send_piece(n, _):
-        j = lax.rem(n + sim, REGION)
-        there = region * REGION + j
-
-        @pl.when(there != sim)
-        def _():
-            pltpu.make_async_remote_copy(
-                src_ref=pack.at[piece_rows(j), :],
-                dst_ref=parts.at[piece_rows(block), :],
-                send_sem=part_send,
-                recv_sem=part_recv,
-                device_id=to(there, grp),
-                device_id_type=MESH,
-            ).start()
-
-        return 0
-
-    lax.fori_loop(0, REGION, send_piece, 0)
+        def send_piece(n, _, h=h):
+            j = 8 * h + lax.rem(n + sim, 8)
+            there = region * REGION + j
+
+            @pl.when(there != sim)
+            def _():
+                pltpu.make_async_remote_copy(
+                    src_ref=pack.at[piece_rows(j), :],
+                    dst_ref=parts.at[piece_rows(block), :],
+                    send_sem=part_send,
+                    recv_sem=part_recv,
+                    device_id=to(there, grp),
+                    device_id_type=MESH,
+                ).start()
+
+            return 0
+
+        lax.fori_loop(0, 8, send_piece, 0)
 
     @pl.when(self_part)
     def _():
@@ -412,14 +422,20 @@
 
     def substrate_rows(k, _):
         r = pl.multiple_of(8 * k, 8)
-        s, lap = laplacian(sbuf, s_up, s_dn, r)
+        rows = pl.ds(r, 8)
+        s, lap = in_plane(sbuf, r)
+        lap = lap + s_up[rows, :] + s_dn[rows, :]
         c = cbuf[pl.ds(pl.multiple_of(r + 8, 8), 8), :]
-        s_new[pl.ds(r, 8), :] = s + DIFF_S * lap - s * c * c + FEED * (1.0 - s)
+        s_new[rows, :] = s + DIFF_S * lap - s * c * c + FEED * (1.0 - s)
         return 0
 
     lax.fori_loop(0, ROWS // 8, substrate_rows, 0, unroll=4)
     store_s = pltpu.make_async_copy(s_new, next_out.at[0, 0], store_sem.at[0])
     store_s.start()
+
+    old = lax.broadcasted_iota(jnp.int32, (256, 256), 0)
+    new = lax.broadcasted_iota(jnp.int32, (256, 256), 1)
+    spread = jnp.where(new == 2 * lax.rem(old, 128) + lax.div(old, 128), 1.0, 0.0).astype(jnp.bfloat16)
 
     def wait_parts(count):
         some = pl.ds(0, count * PIECE)
@@ -449,10 +465,15 @@
     opaque = 1.0 - clear
     channels = [0.5 * (opaque + red), green, 0.5 * (opaque - blue), opaque]
     flat = jnp.concatenate([jnp.concatenate([v[0:4], v[4:8]], axis=1) for v in channels], axis=0)
-    old = lax.broadcasted_iota(jnp.int32, (256, 256), 0)
-    new = lax.broadcasted_iota(jnp.int32, (256, 256), 1)
-    spread = jnp.where(new == 2 * lax.rem(old, 128) + lax.div(old, 128), 1.0, 0.0)
-    mixed = jnp.dot(flat, spread, precision=lax.Precision.HIGHEST, preferred_element_type=jnp.float32)
+    bf16 = jnp.bfloat16
+    high = flat.astype(bf16)
+    rest = flat - high.astype(jnp.float32)
+    middle = rest.astype(bf16)
+    low = (rest - middle.astype(jnp.float32)).astype(bf16)
+    split = jnp.dot(
+        jnp.concatenate([high, middle, low], axis=0), spread, preferred_element_type=jnp.float32
+    )
+    mixed = split[0:16] + (split[16:32] + split[32:48])
     for ch in range(4):
         for par in range(2):
             for t in range(2):
@@ -511,7 +532,7 @@
             collective_id=0, has_side_effects=True, vmem_limit_bytes=32 * 1024 * 1024
         ),
         cost_estimate=pl.CostEstimate(flops=20_000_000, bytes_accessed=4_000_000, transcendentals=2_000_000),
-    )(species)
+    )(pltpu.with_memory_space_constraint(species, pltpu.HBM))
     return fresh, frame
 
 

time: 60.6 us -> 61.9 us (1.021)
  the two profiles are of different devices: /device:TPU:217 before, /device:TPU:9 now
where the time goes in v4:
time: 61.9 us; the launch traced here: 61.8 us
  Pallas kernels  59.5 us (96%)
  local copies, waits for them, and re-layouts  1.58 us (3%)
  between operations  0.64 us (1%)
    pallas_call x1, Pallas kernels, shards(): pl.pallas_call(kernel, out_shape=(jax.ShapeDtypeStruct((2, 1, ROWS, COLS)...  59.5 us
    unnamed x2, local copies, waits for them, and re-layouts  1.58 us

profile of v4, /device:TPU:9, one launch (start us, length us, event | category | flops | bytes accessed | tf_op | source)
XLA Modules:
  0.0 61.8 jit_solution(2439839112945225585)
XLA Ops:
  0.6 59.5 %shard_map.30 = (f32[2,1,128,1024]{3,2,1,0:T(8,128)S(1)}, f32[4,2,512]{2,1,0:T(2,128)S(1)}) custom-call(f32[2,1,128,1024]{3,2,1,0:T(8,128)} %species.1), custom_call_target="tpu_custom_call" | custom-call | flops 20000000 | bytes 4000000 | tf_op jit(solution)/shard_map/pallas_call | solution.py:511
  60.2 1.0 %copy.5 = f32[2,1,128,1024]{3,2,1,0:T(8,128)} copy(f32[2,1,128,1024]{3,2,1,0:T(8,128)S(1)} %get-tuple-element.4) | data formatting | bytes 2097152
  61.2 0.6 copy.6

commit v5 on v4

--- a/solution.py
+++ b/solution.py
@@ -130,7 +130,7 @@
     def halo(i, way, rows):
         target = ((s_up, s_dn), (c_up, c_dn))[i][way]
         return lambda chunk: pltpu.make_async_remote_copy(
-            src_ref=species.at[i, 0, rows, :],
+            src_ref=(sbuf, cbuf)[i].at[pl.ds(pl.multiple_of(rows.start + 8, 8), rows.size), :],
             dst_ref=target.at[rows, :],
             send_sem=halo_send.at[i, way],
             recv_sem=halo_recv.at[i, way, chunk],
@@ -158,8 +158,8 @@
 
         return 0
 
+    loads[1].wait()
     lax.fori_loop(0, CHUNKS, send_catalyst, 0)
-    loads[1].wait()
     loads[0].wait()
 
     def catalyst_rows(i, _):
@@ -272,14 +272,6 @@
     store_c = pltpu.make_async_copy(c_new, next_out.at[1, 0], store_sem.at[1])
     store_c.start()
 
-    @pl.when(has_next)
-    def _():
-        halo(0, 0, whole)(0).start()
-
-    @pl.when(has_prev)
-    def _():
-        halo(0, 1, whole)(0).start()
-
     def wait_mixed(count, t):
         some = pl.ds(0, count * SLOT)
         return pltpu.make_async_remote_copy(
@@ -303,6 +295,14 @@
         @pl.when(t_now != team)
         def _():
             wait_mixed(TEAM, t_now).wait_recv()
+
+        @pl.when((i == 3) & has_next)
+        def _():
+            halo(0, 0, whole)(0).start()
+
+        @pl.when((i == 3) & has_prev)
+        def _():
+            halo(0, 1, whole)(0).start()
 
         base = t_now * (TEAM * SLOT)
         sides = jnp.concatenate(

time: 61.9 us -> 67 us (1.082)
  the two profiles are of different devices: /device:TPU:9 before, /device:TPU:1 now
where the time goes in v5:
time: 67 us; the launch traced here: 66.9 us
  Pallas kernels  64.7 us (97%)
  local copies, waits for them, and re-layouts  1.58 us (2%)
    pallas_call x1, Pallas kernels, shards(): pl.pallas_call(kernel, out_shape=(jax.ShapeDtypeStruct((2, 1, ROWS, COLS)...  64.7 us
    unnamed x2, local copies, waits for them, and re-layouts  1.58 us

profile of v5, /device:TPU:1, one launch (start us, length us, event | category | flops | bytes accessed | tf_op | source)
XLA Modules:
  0.0 66.9 jit_solution(11372868107378499588)
XLA Ops:
  0.6 64.7 %shard_map.30 = (f32[2,1,128,1024]{3,2,1,0:T(8,128)S(1)}, f32[4,2,512]{2,1,0:T(2,128)S(1)}) custom-call(f32[2,1,128,1024]{3,2,1,0:T(8,128)} %species.1), custom_call_target="tpu_custom_call" | custom-call | flops 20000000 | bytes 4000000 | tf_op jit(solution)/shard_map/pallas_call | solution.py:511
  65.3 1.0 %copy.5 = f32[2,1,128,1024]{3,2,1,0:T(8,128)} copy(f32[2,1,128,1024]{3,2,1,0:T(8,128)S(1)} %get-tuple-element.4) | data formatting | bytes 2097152
  66.3 0.6 copy.6

commit v6 on v4

--- a/solution.py
+++ b/solution.py
@@ -130,7 +130,7 @@
     def halo(i, way, rows):
         target = ((s_up, s_dn), (c_up, c_dn))[i][way]
         return lambda chunk: pltpu.make_async_remote_copy(
-            src_ref=species.at[i, 0, rows, :],
+            src_ref=(sbuf, cbuf)[i].at[pl.ds(pl.multiple_of(rows.start + 8, 8), rows.size), :],
             dst_ref=target.at[rows, :],
             send_sem=halo_send.at[i, way],
             recv_sem=halo_recv.at[i, way, chunk],
@@ -158,8 +158,9 @@
 
         return 0
 
-    lax.fori_loop(0, CHUNKS, send_catalyst, 0)
     loads[1].wait()
+    ahead = 2
+    lax.fori_loop(0, ahead, send_catalyst, 0)
     loads[0].wait()
 
     def catalyst_rows(i, _):
@@ -239,6 +240,10 @@
         @pl.when(has_next)
         def _():
             halo(1, 1, chunk_rows(k))(k).wait_recv()
+
+        @pl.when(n < CHUNKS - ahead)
+        def _():
+            send_catalyst(n + ahead, 0)
 
         rim(chunk_at(n + CHUNKS - 2))
         for h in range(CHUNK // 8):

time: 61.9 us -> 68.8 us (1.11)
  the two profiles are of different devices: /device:TPU:9 before, /device:TPU:1 now
where the time goes in v6:
time: 68.8 us; the launch traced here: 68.7 us
  Pallas kernels  66.4 us (97%)
  local copies, waits for them, and re-layouts  1.58 us (2%)
    pallas_call x1, Pallas kernels, shards(): pl.pallas_call(kernel, out_shape=(jax.ShapeDtypeStruct((2, 1, ROWS, COLS)...  66.4 us
    unnamed x2, local copies, waits for them, and re-layouts  1.58 us

profile of v6, /device:TPU:1, one launch (start us, length us, event | category | flops | bytes accessed | tf_op | source)
XLA Modules:
  0.0 68.7 jit_solution(9067172534772215317)
XLA Ops:
  0.6 66.4 %shard_map.30 = (f32[2,1,128,1024]{3,2,1,0:T(8,128)S(1)}, f32[4,2,512]{2,1,0:T(2,128)S(1)}) custom-call(f32[2,1,128,1024]{3,2,1,0:T(8,128)} %species.1), custom_call_target="tpu_custom_call" | custom-call | flops 20000000 | bytes 4000000 | tf_op jit(solution)/shard_map/pallas_call | solution.py:516
  67.1 1.0 %copy.5 = f32[2,1,128,1024]{3,2,1,0:T(8,128)} copy(f32[2,1,128,1024]{3,2,1,0:T(8,128)S(1)} %get-tuple-element.4) | data formatting | bytes 2097152
  68.0 0.6 copy.6

commit v7 on v2

--- a/solution.py
+++ b/solution.py
@@ -376,7 +376,7 @@
         return pl.ds(pl.multiple_of(n * PIECE, PIECE), PIECE)
 
     def send_piece(n, _):
-        j = lax.rem(n + sim, REGION)
+        j = n + lax.rem(region, 2) * (REGION - 1 - 2 * n)
         there = region * REGION + j
 
         @pl.when(there != sim)
@@ -421,6 +421,10 @@
     store_s = pltpu.make_async_copy(s_new, next_out.at[0, 0], store_sem.at[0])
     store_s.start()
 
+    old = lax.broadcasted_iota(jnp.int32, (256, 256), 0)
+    new = lax.broadcasted_iota(jnp.int32, (256, 256), 1)
+    spread = jnp.where(new == 2 * lax.rem(old, 128) + lax.div(old, 128), 1.0, 0.0).astype(jnp.bfloat16)
+
     def wait_parts(count):
         some = pl.ds(0, count * PIECE)
         return pltpu.make_async_remote_copy(
@@ -449,10 +453,15 @@
     opaque = 1.0 - clear
     channels = [0.5 * (opaque + red), green, 0.5 * (opaque - blue), opaque]
     flat = jnp.concatenate([jnp.concatenate([v[0:4], v[4:8]], axis=1) for v in channels], axis=0)
-    old = lax.broadcasted_iota(jnp.int32, (256, 256), 0)
-    new = lax.broadcasted_iota(jnp.int32, (256, 256), 1)
-    spread = jnp.where(new == 2 * lax.rem(old, 128) + lax.div(old, 128), 1.0, 0.0)
-    mixed = jnp.dot(flat, spread, precision=lax.Precision.HIGHEST, preferred_element_type=jnp.float32)
+    bf16 = jnp.bfloat16
+    high = flat.astype(bf16)
+    rest = flat - high.astype(jnp.float32)
+    middle = rest.astype(bf16)
+    low = (rest - middle.astype(jnp.float32)).astype(bf16)
+    split = jnp.dot(
+        jnp.concatenate([high, middle, low], axis=0), spread, preferred_element_type=jnp.float32
+    )
+    mixed = split[0:16] + (split[16:32] + split[32:48])
     for ch in range(4):
         for par in range(2):
             for t in range(2):
@@ -511,7 +520,7 @@
             collective_id=0, has_side_effects=True, vmem_limit_bytes=32 * 1024 * 1024
         ),
         cost_estimate=pl.CostEstimate(flops=20_000_000, bytes_accessed=4_000_000, transcendentals=2_000_000),
-    )(species)
+    )(pltpu.with_memory_space_constraint(species, pltpu.HBM))
     return fresh, frame
 
 

time: 60.6 us -> 60.4 us (level)
  the two profiles are of different devices: /device:TPU:217 before, /device:TPU:89 now
where the time goes in v7:
time: 60.4 us; the launch traced here: 60.3 us
  Pallas kernels  58.1 us (96%)
  local copies, waits for them, and re-layouts  1.58 us (3%)
  between operations  0.64 us (1%)
    pallas_call x1, Pallas kernels, shards(): pl.pallas_call(kernel, out_shape=(jax.ShapeDtypeStruct((2, 1, ROWS, COLS)...  58.1 us
    unnamed x2, local copies, waits for them, and re-layouts  1.58 us

profile of v7, /device:TPU:89, one launch (start us, length us, event | category | flops | bytes accessed | tf_op | source)
XLA Modules:
  0.0 60.3 jit_solution(12538698735768067936)
XLA Ops:
  0.6 58.1 %shard_map.30 = (f32[2,1,128,1024]{3,2,1,0:T(8,128)S(1)}, f32[4,2,512]{2,1,0:T(2,128)S(1)}) custom-call(f32[2,1,128,1024]{3,2,1,0:T(8,128)} %species.1), custom_call_target="tpu_custom_call" | custom-call | flops 20000000 | bytes 4000000 | tf_op jit(solution)/shard_map/pallas_call | solution.py:499
  58.7 1.0 %copy.5 = f32[2,1,128,1024]{3,2,1,0:T(8,128)} copy(f32[2,1,128,1024]{3,2,1,0:T(8,128)S(1)} %get-tuple-element.4) | data formatting | bytes 2097152
  59.7 0.6 %copy.6 = f32[4,2,512]{2,1,0:T(2,128)} copy(f32[4,2,512]{2,1,0:T(2,128)S(1)} %get-tuple-element.5) | data formatting | bytes 32768

commit v8 on v7

--- a/solution.py
+++ b/solution.py
@@ -44,8 +44,8 @@
 
 def kernel(
     species, next_out, frame_out,
-    sbuf, cbuf, s_up, s_dn, c_up, c_dn, s_new, c_new, edge_cols, sendbuf, recvbuf, totals, pack, parts,
-    load_sem, store_sem, halo_send, halo_recv, own_sem, mix_send, mix_recv, part_own, part_send, part_recv,
+    sbuf, cbuf, s_up, s_dn, c_up, c_dn, passing, c_new, edge_cols, sendbuf, recvbuf, totals, pack, parts,
+    load_sem, halo_send, halo_recv, relay_send, relay_recv, own_sem, mix_send, mix_recv, part_own, part_send, part_recv,
 ):
     sim, grp = lax.axis_index("sim"), lax.axis_index("grp")
     plane = sim * GRP + grp
@@ -81,6 +81,15 @@
     has_prev, has_next = plane > 0, plane < SIMS * GRP - 1
     prev = to(lax.div(plane - 1, GRP), lax.rem(plane - 1 + GRP, GRP))
     nxt = to(lax.div(plane + 1, GRP), lax.rem(plane + 1, GRP))
+
+    odd = lax.rem(sim, 2)
+    partner = to(sim + 2 * odd - 1, grp)
+    crossing = (sim + odd > 0) & (sim + odd < SIMS)
+    is_a, is_b = crossing & (odd == 1) & (grp == GRP - 1), crossing & (odd == 0) & (grp == 0)
+    is_relay = crossing & (((odd == 0) & (grp == GRP - 1)) | ((odd == 1) & (grp == 0)))
+    passes_up = is_relay & (odd == 0)
+    passes_down = is_relay & (odd == 1)
+    relayed_to = to(sim, GRP - 1 - grp)
     barrier = pltpu.get_barrier_semaphore()
 
     @pl.when(has_prev)
@@ -90,6 +99,10 @@
     @pl.when(has_next)
     def _():
         pl.semaphore_signal(barrier, inc=1, device_id=nxt, device_id_type=MESH)
+
+    @pl.when(is_relay)
+    def _():
+        pl.semaphore_signal(barrier, inc=1, device_id=partner, device_id_type=MESH)
 
     def greet_member(d, _):
         other = lax.rem(seat + d, MEMBERS)
@@ -126,7 +139,8 @@
 
     self_part = lax.div(sim, REGION) == region
     expected = MEMBERS - 1 + BLOCKS - self_part.astype(jnp.int32)
-    expected = expected + has_prev.astype(jnp.int32) + has_next.astype(jnp.int32)
+    for wanted in (has_prev, has_next, is_a, is_b):
+        expected = expected + wanted.astype(jnp.int32)
     pl.semaphore_wait(barrier, expected)
 
     def halo(i, way, rows):
@@ -232,6 +246,7 @@
             s = sbuf[pl.ds(pl.multiple_of(r + 8, 8), 8), :]
             new = c + DIFF_C * lap + s * c * c - (FEED + KILL) * c
             c_new[pl.ds(r, 8), :] = new
+            next_out[1, 0, pl.ds(r, 8), :] = new
             columns = jnp.zeros((8, 128), jnp.float32)
             for i, (tile, at) in enumerate(beside):
                 moved = pltpu.roll(new[:, tile * 128 : tile * 128 + 128], (i - at) % 128, 1)
@@ -261,16 +276,37 @@
     last_rims = lambda n, _: (send_rim(lax.rem(first + CHUNKS - 1 + n, CHUNKS)), 0)[1]
     lax.fori_loop(0, 2, last_rims, 0)
 
-    store_c = pltpu.make_async_copy(c_new, next_out.at[1, 0], store_sem.at[1])
-    store_c.start()
-
-    @pl.when(has_next)
-    def _():
-        halo(0, 0, whole)(0).start()
-
-    @pl.when(has_prev)
-    def _():
-        halo(0, 1, whole)(0).start()
+    near_half, far_half = pl.ds(0, ROWS // 2), pl.ds(ROWS // 2, ROWS // 2)
+
+    def to_relay(way):
+        return pltpu.make_async_remote_copy(
+            src_ref=species.at[0, 0, far_half, :],
+            dst_ref=passing,
+            send_sem=halo_send.at[0, way],
+            recv_sem=relay_recv,
+            device_id=partner,
+            device_id_type=MESH,
+        )
+
+    def from_relay(way):
+        return pltpu.make_async_remote_copy(
+            src_ref=passing,
+            dst_ref=(s_up, s_dn)[way].at[far_half, :],
+            send_sem=relay_send,
+            recv_sem=halo_recv.at[0, way, 0],
+            device_id=relayed_to,
+            device_id_type=MESH,
+        )
+
+    for way, wanted, end in ((0, has_next, is_a), (1, has_prev, is_b)):
+        @pl.when(wanted & jnp.logical_not(end))
+        def _(way=way):
+            halo(0, way, whole)(0).start()
+
+        @pl.when(end)
+        def _(way=way):
+            to_relay(way).start()
+            halo(0, way, near_half)(0).start()
 
     def wait_mixed(count, t):
         some = pl.ds(0, count * SLOT)
@@ -402,6 +438,12 @@
         mine.start()
         mine.wait()
 
+    for way, wanted in ((0, passes_up), (1, passes_down)):
+        @pl.when(wanted)
+        def _(way=way):
+            to_relay(way).wait_recv()
+            from_relay(way).start()
+
     @pl.when(has_prev)
     def _():
         halo(0, 0, whole)(0).wait_recv()
@@ -414,12 +456,10 @@
         r = pl.multiple_of(8 * k, 8)
         s, lap = laplacian(sbuf, s_up, s_dn, r)
         c = cbuf[pl.ds(pl.multiple_of(r + 8, 8), 8), :]
-        s_new[pl.ds(r, 8), :] = s + DIFF_S * lap - s * c * c + FEED * (1.0 - s)
+        next_out[0, 0, pl.ds(r, 8), :] = s + DIFF_S * lap - s * c * c + FEED * (1.0 - s)
         return 0
 
     lax.fori_loop(0, ROWS // 8, substrate_rows, 0, unroll=4)
-    store_s = pltpu.make_async_copy(s_new, next_out.at[0, 0], store_sem.at[0])
-    store_s.start()
 
     old = lax.broadcasted_iota(jnp.int32, (256, 256), 0)
     new = lax.broadcasted_iota(jnp.int32, (256, 256), 1)
@@ -468,6 +508,10 @@
                 n = ch * 4 + par * 2 + t
                 frame_out[ch, par : par + 1, t * 256 : t * 256 + 256] = mixed[n : n + 1]
 
+    @pl.when(is_relay)
+    def _():
+        from_relay(0).wait_send()
+
     for i in range(2):
         @pl.when(has_next)
         def _(i=i):
@@ -486,9 +530,6 @@
     @pl.when(jnp.logical_not(self_part))
     def _():
         wait_parts(BLOCKS).wait_send()
-
-    store_c.wait()
-    store_s.wait()
 
 
 def shards(species):
@@ -503,17 +544,17 @@
             jax.ShapeDtypeStruct((4, 2 * ROWS // SIMS, 2 * COLS // GRP), f32),
         ),
         in_specs=[pl.BlockSpec(memory_space=pltpu.HBM)],
-        out_specs=(pl.BlockSpec(memory_space=pl.ANY), pl.BlockSpec(memory_space=pltpu.VMEM)),
+        out_specs=(pl.BlockSpec(memory_space=pltpu.VMEM),) * 2,
         scratch_shapes=[
-            padded, padded, plane, plane, plane, plane,
-            plane, plane,
+            padded, padded, plane, plane, plane, plane, pltpu.VMEM((ROWS // 2, COLS), f32),
+            plane,
             pltpu.VMEM((ROWS + 16, 128), f32),
             pltpu.VMEM((MEMBERS * SLOT, 128), f32),
             pltpu.VMEM((MEMBERS * SLOT, 128), f32),
             pltpu.VMEM((4 * TOTALS, 128), f32),
             pltpu.VMEM((REGION * PIECE, 128), f32),
             pltpu.VMEM((BLOCKS * PIECE, 128), f32),
-            dma((2,)), dma((2,)), dma((2, 2)), dma((2, 2, CHUNKS)),
+            dma((2,)), dma((2, 2)), dma((2, 2, CHUNKS)), dma, dma,
             dma, dma, dma((4,)), dma, dma, dma,
         ],
         compiler_params=pltpu.CompilerParams(

time: 60.4 us -> 59.3 us (0.982)
  the two profiles are of different devices: /device:TPU:89 before, /device:TPU:1 now
where the time goes in v8:
time: 59.3 us; the launch traced here: 59.1 us
  Pallas kernels  56.9 us (96%)
  local copies, waits for them, and re-layouts  1.58 us (3%)
  between operations  0.64 us (1%)
    pallas_call x1, Pallas kernels, shards(): pl.pallas_call(kernel, out_shape=(jax.ShapeDtypeStruct((2, 1, ROWS, COLS)...  56.9 us
    unnamed x2, local copies, waits for them, and re-layouts  1.58 us

profile of v8, /device:TPU:1, one launch (start us, length us, event | category | flops | bytes accessed | tf_op | source)
XLA Modules:
  0.0 59.1 jit_solution(17964271103563253208)
XLA Ops:
  0.6 56.9 %shard_map.30 = (f32[2,1,128,1024]{3,2,1,0:T(8,128)S(1)}, f32[4,2,512]{2,1,0:T(2,128)S(1)}) custom-call(f32[2,1,128,1024]{3,2,1,0:T(8,128)} %species.1), custom_call_target="tpu_custom_call" | custom-call | flops 20000000 | bytes 4000000 | tf_op jit(solution)/shard_map/pallas_call | solution.py:540
  57.5 1.0 %copy.5 = f32[2,1,128,1024]{3,2,1,0:T(8,128)} copy(f32[2,1,128,1024]{3,2,1,0:T(8,128)S(1)} %get-tuple-element.4) | data formatting | bytes 2097152
  58.5 0.6 %copy.6 = f32[4,2,512]{2,1,0:T(2,128)} copy(f32[4,2,512]{2,1,0:T(2,128)S(1)} %get-tuple-element.5) | data formatting | bytes 32768

commit v9 on v8

--- a/solution.py
+++ b/solution.py
@@ -31,15 +31,13 @@
     return {"sim": sim, "grp": grp}
 
 
-def laplacian(buf, up, dn, r):
+def in_plane(buf, r):
     window = buf[pl.ds(r, 24), :]
     center = window[8:16]
     lane = lax.broadcasted_iota(jnp.int32, (8, COLS), 1)
     left = jnp.where(lane == 0, 0.0, pltpu.roll(center, 1, 1))
     right = jnp.where(lane == COLS - 1, 0.0, pltpu.roll(center, COLS - 1, 1))
-    total = up[pl.ds(r, 8), :] + dn[pl.ds(r, 8), :]
-    total = total + window[7:15] + window[9:17] + left + right
-    return center, total - 6.0 * center
+    return center, window[7:15] + window[9:17] + left + right - 6.0 * center
 
 
 def kernel(
@@ -209,7 +207,7 @@
             def _(away=away):
                 away.start()
 
-    def send_rim(k):
+    def make_rim(k):
         top = c_new[pl.ds(pl.multiple_of(jnp.maximum(k * REGION - 8, 0), 8), 8), :]
         bottom = c_new[pl.ds(pl.multiple_of(jnp.minimum(k * REGION + REGION, ROWS - 8), 8), 8), :]
         above = jnp.where(k == 0, top[0:1], top[7:8])
@@ -225,7 +223,6 @@
             tile = jnp.where(row == 2, below[:, c : c + 128], tile)
             tile = jnp.where(row == 3, below[:, c + 128 : c + 256], tile)
             sendbuf[pl.ds(pl.multiple_of((k * GRP + x) * SLOT + 32, 8), 8), :] = tile
-        send_tiles(k, 32, 8)
 
     first = first_chunk(sim)
 
@@ -242,7 +239,8 @@
 
         for h in range(CHUNK // 8):
             r = pl.multiple_of(k * CHUNK + 8 * h, 8)
-            c, lap = laplacian(cbuf, c_up, c_dn, r)
+            c, lap = in_plane(cbuf, r)
+            lap = lap + c_up[pl.ds(r, 8), :] + c_dn[pl.ds(r, 8), :]
             s = sbuf[pl.ds(pl.multiple_of(r + 8, 8), 8), :]
             new = c + DIFF_C * lap + s * c * c - (FEED + KILL) * c
             c_new[pl.ds(r, 8), :] = new
@@ -268,13 +266,17 @@
 
         @pl.when(n >= 2)
         def _():
-            send_rim(lax.rem(first + n - 1, CHUNKS))
+            make_rim(lax.rem(first + n - 1, CHUNKS))
+            send_tiles(lax.rem(first + n - 1, CHUNKS), 32, 8)
 
         return 0
 
     lax.fori_loop(0, CHUNKS, catalyst_chunk, 0)
-    last_rims = lambda n, _: (send_rim(lax.rem(first + CHUNKS - 1 + n, CHUNKS)), 0)[1]
-    lax.fori_loop(0, 2, last_rims, 0)
+    last_two = [lax.rem(first + CHUNKS - 1 + n, CHUNKS) for n in range(2)]
+    for k in last_two:
+        make_rim(k)
+    for k in last_two:
+        send_tiles(k, 32, 8)
 
     near_half, far_half = pl.ds(0, ROWS // 2), pl.ds(ROWS // 2, ROWS // 2)
 
@@ -331,6 +333,12 @@
         @pl.when(t_now != team)
         def _():
             wait_mixed(TEAM, t_now).wait_recv()
+
+        for way, wanted in ((0, passes_up), (1, passes_down)):
+            @pl.when((i == 3) & wanted)
+            def _(way=way):
+                to_relay(way).wait_recv()
+                from_relay(way).start()
 
         base = t_now * (TEAM * SLOT)
         sides = jnp.concatenate(
@@ -392,6 +400,9 @@
 
     lax.fori_loop(0, 4, render, 0)
 
+    def piece_rows(n):
+        return pl.ds(pl.multiple_of(n * PIECE, PIECE), PIECE)
+
     for h in range(2):
         for par in range(2):
             for cpar in range(2):
@@ -408,27 +419,24 @@
                         at = 8 * h * PIECE + ch * 8 + cpar * 4 + par * 2 + t
                         pack[pl.ds(at, 8, stride=PIECE), :] = value
 
-    def piece_rows(n):
-        return pl.ds(pl.multiple_of(n * PIECE, PIECE), PIECE)
-
-    def send_piece(n, _):
-        j = n + lax.rem(region, 2) * (REGION - 1 - 2 * n)
-        there = region * REGION + j
-
-        @pl.when(there != sim)
-        def _():
-            pltpu.make_async_remote_copy(
-                src_ref=pack.at[piece_rows(j), :],
-                dst_ref=parts.at[piece_rows(block), :],
-                send_sem=part_send,
-                recv_sem=part_recv,
-                device_id=to(there, grp),
-                device_id_type=MESH,
-            ).start()
-
-        return 0
-
-    lax.fori_loop(0, REGION, send_piece, 0)
+        def send_piece(n, _, h=h):
+            j = 8 * h + n
+            there = region * REGION + j
+
+            @pl.when(there != sim)
+            def _():
+                pltpu.make_async_remote_copy(
+                    src_ref=pack.at[piece_rows(j), :],
+                    dst_ref=parts.at[piece_rows(block), :],
+                    send_sem=part_send,
+                    recv_sem=part_recv,
+                    device_id=to(there, grp),
+                    device_id_type=MESH,
+                ).start()
+
+            return 0
+
+        lax.fori_loop(0, 8, send_piece, 0)
 
     @pl.when(self_part)
     def _():
@@ -438,25 +446,26 @@
         mine.start()
         mine.wait()
 
-    for way, wanted in ((0, passes_up), (1, passes_down)):
-        @pl.when(wanted)
-        def _(way=way):
-            to_relay(way).wait_recv()
-            from_relay(way).start()
-
-    @pl.when(has_prev)
-    def _():
-        halo(0, 0, whole)(0).wait_recv()
-
-    @pl.when(has_next)
-    def _():
-        halo(0, 1, whole)(0).wait_recv()
-
-    def substrate_rows(k, _):
+    def substrate_part(k, _):
         r = pl.multiple_of(8 * k, 8)
-        s, lap = laplacian(sbuf, s_up, s_dn, r)
+        s, lap = in_plane(sbuf, r)
         c = cbuf[pl.ds(pl.multiple_of(r + 8, 8), 8), :]
         next_out[0, 0, pl.ds(r, 8), :] = s + DIFF_S * lap - s * c * c + FEED * (1.0 - s)
+        return 0
+
+    lax.fori_loop(0, ROWS // 8, substrate_part, 0, unroll=4)
+
+    @pl.when(has_prev)
+    def _():
+        halo(0, 0, whole)(0).wait_recv()
+
+    @pl.when(has_next)
+    def _():
+        halo(0, 1, whole)(0).wait_recv()
+
+    def substrate_rows(k, _):
+        rows = pl.ds(pl.multiple_of(8 * k, 8), 8)
+        next_out[0, 0, rows, :] = next_out[0, 0, rows, :] + DIFF_S * (s_up[rows, :] + s_dn[rows, :])
         return 0
 
     lax.fori_loop(0, ROWS // 8, substrate_rows, 0, unroll=4)

time: 59.3 us -> 58.5 us (0.987); the launches traced: 59.1 us -> 57.5 us
  Pallas kernels: 56.9 us -> 55.3 us
    pallas_call x1, Pallas kernels: 56.9 us -> 55.3 us  [shards(): pl.pallas_call(kernel, out_shape=(jax.ShapeDtypeStruct((2, 1, ROWS, COLS)...]
where the time goes in v9:
time: 58.5 us; the launch traced here: 57.5 us
  Pallas kernels  55.3 us (95%)
  local copies, waits for them, and re-layouts  1.58 us (3%)
  between operations  0.64 us (1%)
    pallas_call x1, Pallas kernels, shards(): pl.pallas_call(kernel, out_shape=(jax.ShapeDtypeStruct((2, 1, ROWS, COLS)...  55.3 us
    unnamed x2, local copies, waits for them, and re-layouts  1.58 us

profile of v9, /device:TPU:1, one launch (start us, length us, event | category | flops | bytes accessed | tf_op | source)
XLA Modules:
  0.0 57.5 jit_solution(4127902160210466281)
XLA Ops:
  0.6 55.3 %shard_map.30 = (f32[2,1,128,1024]{3,2,1,0:T(8,128)S(1)}, f32[4,2,512]{2,1,0:T(2,128)S(1)}) custom-call(f32[2,1,128,1024]{3,2,1,0:T(8,128)} %species.1), custom_call_target="tpu_custom_call" | custom-call | flops 20000000 | bytes 4000000 | tf_op jit(solution)/shard_map/pallas_call | solution.py:549
  55.9 1.0 %copy.5 = f32[2,1,128,1024]{3,2,1,0:T(8,128)} copy(f32[2,1,128,1024]{3,2,1,0:T(8,128)S(1)} %get-tuple-element.4) | data formatting | bytes 2097152
  56.9 0.6 %copy.6 = f32[4,2,512]{2,1,0:T(2,128)} copy(f32[4,2,512]{2,1,0:T(2,128)S(1)} %get-tuple-element.5) | data formatting | bytes 32768

commit v10 on v9

--- a/solution.py
+++ b/solution.py
@@ -226,23 +226,30 @@
 
     first = first_chunk(sim)
 
-    def catalyst_chunk(n, _):
-        k = lax.rem(first + n, CHUNKS)
-
-        @pl.when(has_prev)
-        def _():
-            halo(1, 0, chunk_rows(k))(k).wait_recv()
-
-        @pl.when(has_next)
-        def _():
-            halo(1, 1, chunk_rows(k))(k).wait_recv()
-
+    def own_part(k):
         for h in range(CHUNK // 8):
             r = pl.multiple_of(k * CHUNK + 8 * h, 8)
             c, lap = in_plane(cbuf, r)
-            lap = lap + c_up[pl.ds(r, 8), :] + c_dn[pl.ds(r, 8), :]
             s = sbuf[pl.ds(pl.multiple_of(r + 8, 8), 8), :]
-            new = c + DIFF_C * lap + s * c * c - (FEED + KILL) * c
+            c_new[pl.ds(r, 8), :] = c + DIFF_C * lap + s * c * c - (FEED + KILL) * c
+
+    own_part(first)
+
+    def catalyst_chunk(n, _):
+        k = lax.rem(first + n, CHUNKS)
+
+        @pl.when(has_prev)
+        def _():
+            halo(1, 0, chunk_rows(k))(k).wait_recv()
+
+        @pl.when(has_next)
+        def _():
+            halo(1, 1, chunk_rows(k))(k).wait_recv()
+
+        for h in range(CHUNK // 8):
+            r = pl.multiple_of(k * CHUNK + 8 * h, 8)
+            rows = pl.ds(r, 8)
+            new = c_new[rows, :] + DIFF_C * (c_up[rows, :] + c_dn[rows, :])
             c_new[pl.ds(r, 8), :] = new
             next_out[1, 0, pl.ds(r, 8), :] = new
             columns = jnp.zeros((8, 128), jnp.float32)
@@ -269,6 +276,10 @@
             make_rim(lax.rem(first + n - 1, CHUNKS))
             send_tiles(lax.rem(first + n - 1, CHUNKS), 32, 8)
 
+        @pl.when(n < CHUNKS - 1)
+        def _():
+            own_part(lax.rem(first + n + 1, CHUNKS))
+
         return 0
 
     lax.fori_loop(0, CHUNKS, catalyst_chunk, 0)
@@ -278,11 +289,9 @@
     for k in last_two:
         send_tiles(k, 32, 8)
 
-    near_half, far_half = pl.ds(0, ROWS // 2), pl.ds(ROWS // 2, ROWS // 2)
-
     def to_relay(way):
         return pltpu.make_async_remote_copy(
-            src_ref=species.at[0, 0, far_half, :],
+            src_ref=species.at[0, 0],
             dst_ref=passing,
             send_sem=halo_send.at[0, way],
             recv_sem=relay_recv,
@@ -293,7 +302,7 @@
     def from_relay(way):
         return pltpu.make_async_remote_copy(
             src_ref=passing,
-            dst_ref=(s_up, s_dn)[way].at[far_half, :],
+            dst_ref=(s_up, s_dn)[way],
             send_sem=relay_send,
             recv_sem=halo_recv.at[0, way, 0],
             device_id=relayed_to,
@@ -308,7 +317,6 @@
         @pl.when(end)
         def _(way=way):
             to_relay(way).start()
-            halo(0, way, near_half)(0).start()
 
     def wait_mixed(count, t):
         some = pl.ds(0, count * SLOT)
@@ -555,7 +563,7 @@
         in_specs=[pl.BlockSpec(memory_space=pltpu.HBM)],
         out_specs=(pl.BlockSpec(memory_space=pltpu.VMEM),) * 2,
         scratch_shapes=[
-            padded, padded, plane, plane, plane, plane, pltpu.VMEM((ROWS // 2, COLS), f32),
+            padded, padded, plane, plane, plane, plane, plane,
             plane,
             pltpu.VMEM((ROWS + 16, 128), f32),
             pltpu.VMEM((MEMBERS * SLOT, 128), f32),

time: 58.5 us -> 64.2 us (1.097)
  the two profiles are of different devices: /device:TPU:1 before, /device:TPU:7 now
where the time goes in v10:
time: 64.2 us; the launch traced here: 64.1 us
  Pallas kernels  61.8 us (96%)
  local copies, waits for them, and re-layouts  1.58 us (2%)
    pallas_call x1, Pallas kernels, shards(): pl.pallas_call(kernel, out_shape=(jax.ShapeDtypeStruct((2, 1, ROWS, COLS)...  61.8 us
    unnamed x2, local copies, waits for them, and re-layouts  1.58 us

profile of v10, /device:TPU:7, one launch (start us, length us, event | category | flops | bytes accessed | tf_op | source)
XLA Modules:
  0.0 64.1 jit_solution(13937600913000137569)
XLA Ops:
  0.6 61.8 %shard_map.30 = (f32[2,1,128,1024]{3,2,1,0:T(8,128)S(1)}, f32[4,2,512]{2,1,0:T(2,128)S(1)}) custom-call(f32[2,1,128,1024]{3,2,1,0:T(8,128)} %species.1), custom_call_target="tpu_custom_call" | custom-call | flops 20000000 | bytes 4000000 | tf_op jit(solution)/shard_map/pallas_call | solution.py:557
  62.5 1.0 %copy.5 = f32[2,1,128,1024]{3,2,1,0:T(8,128)} copy(f32[2,1,128,1024]{3,2,1,0:T(8,128)S(1)} %get-tuple-element.4) | data formatting | bytes 2097152
  63.5 0.6 copy.6

commit v11 on v9

--- a/solution.py
+++ b/solution.py
@@ -66,7 +66,7 @@
     team = lax.div(member, 2)
 
     def source(b):
-        t = lax.div(b, 4) + lax.rem(b, 4)
+        t = b // 4 + b % 4
         return b * SUB + member_of(lax.div(sim, REGION), t)
 
     loads = [
@@ -89,6 +89,13 @@
     passes_down = is_relay & (odd == 1)
     relayed_to = to(sim, GRP - 1 - grp)
     barrier = pltpu.get_barrier_semaphore()
+    for b in range(BLOCKS):
+        there = source(b)
+
+        @pl.when(there != sim)
+        def _(there=there):
+            pl.semaphore_signal(barrier, inc=1, device_id=to(there, grp), device_id_type=MESH)
+
 
     @pl.when(has_prev)
     def _():
@@ -109,17 +116,6 @@
         return 0
 
     lax.fori_loop(1, MEMBERS, greet_member, 0)
-
-    def greet_source(b, _):
-        there = source(b)
-
-        @pl.when(there != sim)
-        def _():
-            pl.semaphore_signal(barrier, inc=1, device_id=to(there, grp), device_id_type=MESH)
-
-        return 0
-
-    lax.fori_loop(0, BLOCKS, greet_source, 0)
 
     for buf in (sbuf, cbuf):
         buf[0:8, :] = jnp.zeros((8, COLS), jnp.float32)

time: 58.5 us -> 58.5 us (level); the launches traced: 57.5 us -> 58.4 us
  Pallas kernels: 55.3 us -> 56.2 us
    pallas_call x1, Pallas kernels: 55.3 us -> 56.2 us  [shards(): pl.pallas_call(kernel, out_shape=(jax.ShapeDtypeStruct((2, 1, ROWS, COLS)...]
where the time goes in v11:
time: 58.5 us; the launch traced here: 58.4 us
  Pallas kernels  56.2 us (96%)
  local copies, waits for them, and re-layouts  1.58 us (3%)
  between operations  0.64 us (1%)
    pallas_call x1, Pallas kernels, shards(): pl.pallas_call(kernel, out_shape=(jax.ShapeDtypeStruct((2, 1, ROWS, COLS)...  56.2 us
    unnamed x2, local copies, waits for them, and re-layouts  1.58 us

profile of v11, /device:TPU:1, one launch (start us, length us, event | category | flops | bytes accessed | tf_op | source)
XLA Modules:
  0.0 58.4 jit_solution(5160895755578162470)
XLA Ops:
  0.6 56.2 %shard_map.30 = (f32[2,1,128,1024]{3,2,1,0:T(8,128)S(1)}, f32[4,2,512]{2,1,0:T(2,128)S(1)}) custom-call(f32[2,1,128,1024]{3,2,1,0:T(8,128)} %species.1), custom_call_target="tpu_custom_call" | custom-call | flops 20000000 | bytes 4000000 | tf_op jit(solution)/shard_map/pallas_call | solution.py:545
  56.8 1.0 %copy.5 = f32[2,1,128,1024]{3,2,1,0:T(8,128)} copy(f32[2,1,128,1024]{3,2,1,0:T(8,128)S(1)} %get-tuple-element.4) | data formatting | bytes 2097152
  57.8 0.6 %copy.6 = f32[4,2,512]{2,1,0:T(2,128)} copy(f32[4,2,512]{2,1,0:T(2,128)S(1)} %get-tuple-element.5) | data formatting | bytes 32768

commit v12 on v11

--- a/solution.py
+++ b/solution.py
@@ -331,7 +331,7 @@
             wait_mixed(TEAM, t_now).wait_recv()
 
         for way, wanted in ((0, passes_up), (1, passes_down)):
-            @pl.when((i == 3) & wanted)
+            @pl.when((i == 2) & wanted)
             def _(way=way):
                 to_relay(way).wait_recv()
                 from_relay(way).start()

time: 58.5 us -> 58.4 us (level)
  no operation moved by 1% of the time
where the time goes in v12:
time: 58.4 us; the launch traced here: 57.9 us
  Pallas kernels  55.7 us (95%)
  local copies, waits for them, and re-layouts  1.58 us (3%)
  between operations  0.64 us (1%)
    pallas_call x1, Pallas kernels, shards(): pl.pallas_call(kernel, out_shape=(jax.ShapeDtypeStruct((2, 1, ROWS, COLS)...  55.7 us
    unnamed x2, local copies, waits for them, and re-layouts  1.58 us

profile of v12, /device:TPU:1, one launch (start us, length us, event | category | flops | bytes accessed | tf_op | source)
XLA Modules:
  0.0 57.9 jit_solution(16942009040941324958)
XLA Ops:
  0.6 55.7 %shard_map.30 = (f32[2,1,128,1024]{3,2,1,0:T(8,128)S(1)}, f32[4,2,512]{2,1,0:T(2,128)S(1)}) custom-call(f32[2,1,128,1024]{3,2,1,0:T(8,128)} %species.1), custom_call_target="tpu_custom_call" | custom-call | flops 20000000 | bytes 4000000 | tf_op jit(solution)/shard_map/pallas_call | solution.py:545
  56.3 1.0 %copy.5 = f32[2,1,128,1024]{3,2,1,0:T(8,128)} copy(f32[2,1,128,1024]{3,2,1,0:T(8,128)S(1)} %get-tuple-element.4) | data formatting | bytes 2097152
  57.3 0.6 %copy.6 = f32[4,2,512]{2,1,0:T(2,128)} copy(f32[4,2,512]{2,1,0:T(2,128)S(1)} %get-tuple-element.5) | data formatting | bytes 32768
